TPU v7x, 256 devices: a whole 4x4x8 slice. The times are simulated.
256 devices in a mesh: bulk: 32 (over x, z_lo, core), row: 8 (over y, z_hi).
Axes of the slice: x: 4, y: 4, z: 8 (z_hi: 2, z_lo: 4; z = z_hi * 4 + z_lo), core: 2. Of those that a mesh axis runs over, the one named last changes fastest.
Arguments:
- charge: float32 [512, 256, 512], P('row', 'bulk'), may hold values from -6 to 6
- green_table: float32 [8, 256, 256], replicated, may hold values from -1 to 2
- shells: int32 [512, 512], P('bulk'), may hold values from 0 to 7, as said below
- planes: int32 [4], replicated, may hold values from 0 to 255
Outputs:
- potential: float32 [512, 256, 512], P('row', 'bulk')
- electrodes: float32 [4, 512, 512], P(None, 'row', 'bulk')
Inputs may be any that keep to these rules, and one draw needn't show every extreme that they name: shells[kx, ky] depends only on fx * fx + fy * fy, with fx and fy the signed frequencies of kx and ky, and does not fall as it grows.
All inputs are finite; a program needn't handle non-finite values.
Results may differ from a plain program's by a relative error of at most 0.0003.
Values sent between devices are 32-bit elements; how exact they have to be, the bound alone decides.
A program may use at most 128 MiB of HBM per device.

v0:
```python
import math

import jax
import jax.numpy as jnp
from jax import lax
from jax.sharding import PartitionSpec as P

exact_mode = lax.Precision.HIGHEST
full_turn = 2.0 * math.pi


def phase_table(length, row_index, col_index):
    residue = row_index[:, None] * col_index[None, :] % length
    angles = residue.astype(jnp.float32) * (full_turn / length)
    return (jnp.cos(angles), jnp.sin(angles))


def apply_green(green_table, columns, labels):
    full_z, halves, kx_local, ky_local = columns.shape
    column_count = halves * kx_local * ky_local
    flat_data = columns.reshape(full_z, column_count)
    flat_labels = labels.reshape(column_count)
    sort_order = jnp.argsort(flat_labels, stable=True)
    ranked = flat_labels[sort_order]
    arranged = jnp.take(flat_data, sort_order, axis=1)
    tile_count = 1
    while (
        tile_count < 8
        and column_count % (2 * tile_count) == 0
        and (column_count // (2 * tile_count) >= 128)
    ):
        tile_count = 2 * tile_count
    tile_width = column_count // tile_count
    results = []
    for tile_index in range(tile_count):
        tile_data = arranged[:, tile_index * tile_width : (tile_index + 1) * tile_width]
        tile_shells = ranked[tile_index * tile_width : (tile_index + 1) * tile_width]

        def add_shell(shell_index, running, tile_data=tile_data, tile_shells=tile_shells):
            matrix = lax.dynamic_index_in_dim(green_table, shell_index, 0, keepdims=False)
            picked = jnp.where(tile_shells[None, :] == shell_index, tile_data, 0.0)
            return running + jnp.dot(matrix, picked, precision=exact_mode)

        results.append(
            lax.fori_loop(
                tile_shells[0],
                tile_shells[tile_width - 1] + 1,
                add_shell,
                jnp.zeros_like(tile_data),
            )
        )
    solved_sorted = jnp.concatenate(results, axis=1)
    restore = (
        jnp.zeros((column_count,), jnp.int32)
        .at[sort_order]
        .set(jnp.arange(column_count, dtype=jnp.int32))
    )
    return jnp.take(solved_sorted, restore, axis=1).reshape(full_z, halves, kx_local, ky_local)


def local(charge, green_table, shells, planes):
    rows_x, local_z, width_y = charge.shape
    full_x = rows_x * lax.axis_size("row")
    index_y = jnp.arange(width_y, dtype=jnp.int32)
    index_x = jnp.arange(full_x, dtype=jnp.int32)
    cos_y, sin_y = phase_table(width_y, index_y, index_y)
    cos_x, sin_x = phase_table(full_x, index_x, index_x)
    forward_y = jnp.stack([cos_y, -sin_y], axis=1)
    inverse_y = jnp.stack([cos_y, -sin_y]) / width_y
    spectrum = jnp.einsum("xzn,nrk->rxzk", charge, forward_y, precision=exact_mode)
    spectrum = lax.all_to_all(spectrum, "row", split_axis=3, concat_axis=1, tiled=True)
    ky_local = spectrum.shape[3]
    forward_x = jnp.block([[cos_x, sin_x], [-sin_x, cos_x]])
    stacked = spectrum.reshape(2 * full_x, local_z, ky_local)
    planes_k = jnp.einsum("ab,bzk->zak", forward_x, stacked, precision=exact_mode).reshape(
        local_z, 2, full_x, ky_local
    )
    columns = lax.all_to_all(planes_k, "bulk", split_axis=2, concat_axis=0, tiled=True)
    kx_local = columns.shape[2]
    own = lax.dynamic_slice_in_dim(shells, lax.axis_index("row") * ky_local, ky_local, 1)
    labels = jnp.broadcast_to(own[None, :, :], (2, kx_local, ky_local))
    solved = apply_green(green_table, columns, labels)
    returned = lax.all_to_all(solved, "bulk", split_axis=0, concat_axis=2, tiled=True)
    inverse_x = jnp.block([[cos_x, -sin_x], [sin_x, cos_x]]) / full_x
    depth = returned.shape[0]
    merged = returned.reshape(depth, 2 * full_x, ky_local)
    spatial_x = jnp.einsum("ab,zbk->azk", inverse_x, merged, precision=exact_mode).reshape(
        2, full_x, depth, ky_local
    )
    arrived = lax.all_to_all(spatial_x, "row", split_axis=1, concat_axis=3, tiled=True)
    real_field = jnp.einsum("rxzk,rkn->xzn", arrived, inverse_y, precision=exact_mode)
    first_plane = lax.axis_index("bulk") * local_z
    selector = (
        planes[:, None] == first_plane + jnp.arange(local_z, dtype=jnp.int32)[None, :]
    ).astype(jnp.float32)
    local_terms = jnp.einsum("pz,xzn->pxn", selector, real_field, precision=exact_mode)
    electrodes = lax.psum_scatter(local_terms, "bulk", scatter_dimension=2, tiled=True)
    return (real_field, electrodes)


def solution(mesh):
    placed = (P("row", "bulk", None), P(), P("bulk", None), P())
    return jax.shard_map(
        local,
        mesh=mesh,
        in_specs=placed,
        out_specs=(P("row", "bulk", None), P(None, "row", "bulk")),
        check_vma=False,
    )
```

profile of v0, /device:TPU:1, one launch (start us, length us, event | category | flops | bytes accessed | tf_op | source)
XLA Modules:
  0.0 800.0 jit_solution(15156729350634625780)
XLA Ops:
  7.2 4.1 sine_negate_fusion.1
  11.3 5.4 fusion.72
  16.7 4.8 copy.54
  21.6 7.2 reshape.292
  28.8 11.9 %all-to-all-start = ((f32[8,1,65536]{2,1,0:T(1,128)}), f32[8,1,65536]{2,1,0:T(1,128)}, u32[]{:S(2)}, u32[]{:S(2)}) async-start(f32[8,1,65536]{2,1,0:T(1,128)} %reshape.292), calls=%async_computation | async-start | bytes 4194304 | tf_op jit(solution)/shard_map/all_to_all | solution.py:71
  44.5 5.3 fusion.102
  49.8 27.1 %all-to-all-done = f32[8,1,65536]{2,1,0:T(1,128)} async-done(((f32[8,1,65536]{2,1,0:T(1,128)}), f32[8,1,65536]{2,1,0:T(1,128)}, u32[]{:S(2)}, u32[]{:S(2)}) %all-to-all-start) | async-done | bytes 2097184 | tf_op jit(solution)/shard_map/all_to_all | solution.py:71
  77.5 8.6 %reduce = f32[8,65536]{1,0:T(8,128)} reduce(f32[8,1,65536]{2,1,0:T(1,128)} %all-to-all-done, f32[]{:T(128)} %broadcast.321), dimensions={1}, to_apply=%all_to_all.46.reduce_sub_computation | reduce | bytes 4194308 | tf_op jit(solution)/shard_map/all_to_all | solution.py:71
  86.0 5.2 reshape.293
  91.2 6.6 copy.95
  97.8 4.9 reshape.236
  102.7 11.6 %fusion.73 = f32[8,1024,64]{1,2,0:T(8,128)} fusion(f32[1024,8,64]{0,2,1:T(8,128)} %reshape.236, f32[512,512]{1,0:T(8,128)} %get-tuple-element.558, f32[512,512]{1,0:T(8,128)S(1)} %fusion.104, f32[512,512]{1,0:T(8,128)S(1)} %get-tuple-element.557), kind=kOutput, calls=%fused_computation.100 | convolution fusion | flops 6445596672 | bytes 7340032 | tf_op jit(solution)/shard_map/ab,bzk->zak/dot_general | solution.py:75
  114.3 4.0 reshape.237
  118.3 6.7 copy.56
  125.0 6.6 reshape.294
  131.6 23.4 %all-to-all-start.1 = ((f32[32,1,16384]{2,1,0:T(1,128)}), f32[32,1,16384]{2,1,0:T(1,128)}, u32[]{:S(2)}, u32[]{:S(2)}) async-start(f32[32,1,16384]{2,1,0:T(1,128)} %reshape.294), calls=%async_computation.1 | async-start | bytes 4194304 | tf_op jit(solution)/shard_map/all_to_all | solution.py:78
  155.3 5.0 sort.17
  160.3 11.8 %gather_fusion = s32[2048]{0:T(1024)S(1)} fusion(s32[2048]{0:T(1024)S(1)} %reshape.235, s32[2048]{0:T(1024)S(1)} %get-tuple-element.532), kind=kCustom, calls=%fused_computation.2 | custom fusion | bytes 24576 | tf_op jit(solution)/shard_map/gather | solution.py:24
  177.7 8.2 %scatter_custom_fusion = s32[2048]{0:T(1024)S(1)} fusion(s32[2048]{0:T(1024)S(1)} %get-tuple-element.531, s32[2048]{0:T(1024)S(1)} %iota.47, s32[]{:T(128)} %constant.121.clone.1), kind=kCustom, calls=%fused_computation.154 | custom fusion | bytes 8196 | tf_op jit(solution)/shard_map/scatter | solution.py:56
  186.0 18.9 %all-to-all-done.1 = f32[32,1,16384]{2,1,0:T(1,128)} async-done(((f32[32,1,16384]{2,1,0:T(1,128)}), f32[32,1,16384]{2,1,0:T(1,128)}, u32[]{:S(2)}, u32[]{:S(2)}) %all-to-all-start.1) | async-done | bytes 2097184 | tf_op jit(solution)/shard_map/all_to_all | solution.py:78
  204.9 7.4 reduce.1
  212.3 4.4 reshape.295
  222.8 5.0 reshape.238
  229.7 8.6 %gather_fusion.1 = f32[2048,256]{1,0:T(8,128)} fusion(f32[256,2048]{0,1:T(8,128)S(1)} %copy.59, s32[2048]{0:T(1024)S(1)} %get-tuple-element.532), kind=kCustom, calls=%fused_computation.clone | custom fusion | bytes 4202496 | tf_op jit(solution)/shard_map/jit(_take)/gather | solution.py:25
  241.4 6.5 while.80
  248.2 6.1 while.81
  256.2 6.3 while.82
  264.5 6.7 while.83
  273.1 6.9 while.84
  281.0 12.2 %while.85 = (s32[]{:T(128)}, f32[256,256]{1,0:T(8,128)S(1)}, s32[]{:T(128)}, f32[8,256,256]{2,1,0:T(8,128)}, s32[256]{0:T(256)S(1)}, /*index=5*/f32[256,256]{1,0:T(8,128)S(1)}, s32[]{:T(128)}, s32[]{:T(128)}, s32[]{:T(128)}) while((s32[]{:T(128)}, f32[256,256]{1,0:T(8,128)S(1)}, s32[]{:T(128)}, f32[8,256,256]{2,1,0:T(8,128)}, ...), condition=%wide.region_12.14_spmd, body=%wide.region_11.13_spmd.sunk | while | flops 201457920 | bytes 1050247 | solution.py:45
  294.2 6.8 while.86
  302.0 6.5 while.87
  310.5 8.6 %gather_fusion.2 = f32[2048,256]{1,0:T(8,128)} fusion(f32[256,2048]{0,1:T(8,128)S(1)} %constant_dynamic-update-slice_fusion, s32[2048]{0:T(1024)S(1)} %fusion.105), kind=kCustom, calls=%fused_computation.1.clone | custom fusion | bytes 4202496 | tf_op jit(solution)/shard_map/jit(_take)/gather | solution.py:58
  321.0 4.5 copy.76
  325.5 5.5 reshape.296
  330.9 6.3 all-to-all-start.2
  339.8 47.1 %all-to-all-done.2 = f32[32,1,16384]{2,1,0:T(1,128)} async-done(((f32[32,1,16384]{2,1,0:T(1,128)}), f32[32,1,16384]{2,1,0:T(1,128)}, u32[]{:S(2)}, u32[]{:S(2)}) %all-to-all-start.2) | async-done | bytes 2097184 | tf_op jit(solution)/shard_map/all_to_all | solution.py:83
  386.9 7.4 reduce.2
  401.2 6.9 fusion.120
  411.9 7.2 reshape.298
  419.2 16.7 %all-to-all-start.3 = ((f32[8,1,65536]{2,1,0:T(1,128)}), f32[8,1,65536]{2,1,0:T(1,128)}, u32[]{:S(2)}, u32[]{:S(2)}) async-start(f32[8,1,65536]{2,1,0:T(1,128)} %reshape.298), calls=%async_computation.3 | async-start | bytes 4194304 | tf_op jit(solution)/shard_map/all_to_all | solution.py:90
  435.9 5.5 sine_negate_fusion
  441.4 43.8 %all-to-all-done.3 = f32[8,1,65536]{2,1,0:T(1,128)} async-done(((f32[8,1,65536]{2,1,0:T(1,128)}), f32[8,1,65536]{2,1,0:T(1,128)}, u32[]{:S(2)}, u32[]{:S(2)}) %all-to-all-start.3) | async-done | bytes 2097184 | tf_op jit(solution)/shard_map/all_to_all | solution.py:90
  485.1 7.2 reduce.3
  496.0 6.6 copy.94
  502.5 5.0 all_to_all.58
  507.6 5.4 fusion.76
  516.3 275.2 %all-reduce.3.cloned.1.call-done = f32[4,64,512]{1,0,2:T(4,128)} async-done(((f32[4,64,512]{1,0,2:T(4,128)}), f32[4,64,512]{1,0,2:T(4,128)}) %all-reduce.3.cloned.1.call-update) | async-done | bytes 524304
  (120 shorter events, 68.8 us)
Async XLA Ops:
  7.2 147.9 %copy-start = (s32[16,512]{1,0:T(8,128)S(1)}, s32[16,512]{1,0:T(8,128)}, u32[]{:S(2)}) copy-start(s32[16,512]{1,0:T(8,128)} %param.24) | copy-start | bytes 98308
  7.2 4.1 copy-start.9
  28.8 48.1 %all-to-all-start = ((f32[8,1,65536]{2,1,0:T(1,128)}), f32[8,1,65536]{2,1,0:T(1,128)}, u32[]{:S(2)}, u32[]{:S(2)}) async-start(f32[8,1,65536]{2,1,0:T(1,128)} %reshape.292), calls=%async_computation | async-start | bytes 4194304 | tf_op jit(solution)/shard_map/all_to_all | solution.py:71
  44.5 58.2 %copy-start.3 = (f32[512,512]{1,0:T(8,128)}, f32[512,512]{1,0:T(8,128)S(1)}, u32[]{:S(2)}) copy-start(f32[512,512]{1,0:T(8,128)S(1)} %fusion.104) | copy-start | bytes 3145732
  49.8 52.9 %copy-start.5 = (f32[512,512]{1,0:T(8,128)}, f32[512,512]{1,0:T(8,128)S(1)}, u32[]{:S(2)}) copy-start(f32[512,512]{1,0:T(8,128)S(1)} %get-tuple-element.557) | copy-start | bytes 3145732
  131.6 73.3 %all-to-all-start.1 = ((f32[32,1,16384]{2,1,0:T(1,128)}), f32[32,1,16384]{2,1,0:T(1,128)}, u32[]{:S(2)}, u32[]{:S(2)}) async-start(f32[32,1,16384]{2,1,0:T(1,128)} %reshape.294), calls=%async_computation.1 | async-start | bytes 4194304 | tf_op jit(solution)/shard_map/all_to_all | solution.py:78
  302.0 7.3 copy-start.10
  302.0 7.4 copy-start.11
  302.0 7.4 copy-start.12
  308.5 1.0 copy-start.13
  309.3 1.0 copy-start.14
  309.3 1.0 copy-start.15
  309.3 1.1 copy-start.16
  330.9 6.3 copy-start.4
  330.9 6.3 copy-start.6
  330.9 6.3 copy-start.7
  330.9 56.0 %all-to-all-start.2 = ((f32[32,1,16384]{2,1,0:T(1,128)}), f32[32,1,16384]{2,1,0:T(1,128)}, u32[]{:S(2)}, u32[]{:S(2)}) async-start(f32[32,1,16384]{2,1,0:T(1,128)} %reshape.296), calls=%async_computation.2 | async-start | bytes 4194304 | tf_op jit(solution)/shard_map/all_to_all | solution.py:83
  397.8 3.5 copy-start.2
  419.2 66.0 %all-to-all-start.3 = ((f32[8,1,65536]{2,1,0:T(1,128)}), f32[8,1,65536]{2,1,0:T(1,128)}, u32[]{:S(2)}, u32[]{:S(2)}) async-start(f32[8,1,65536]{2,1,0:T(1,128)} %reshape.298), calls=%async_computation.3 | async-start | bytes 4194304 | tf_op jit(solution)/shard_map/all_to_all | solution.py:90
  435.8 355.7 %all-reduce.3.cloned.1.call-start = ((), (), s32[]{:S(2)}) async-start(), calls=%async_computation.4 | async-start | bytes 2097152
  507.5 5.5 copy-start.17
  507.5 285.4 %copy-start.1 = (s32[16,512]{1,0:T(8,128)S(1)}, s32[16,512]{1,0:T(8,128)}, u32[]{:S(2)}) copy-start(s32[16,512]{1,0:T(8,128)} %param.24) | copy-start | bytes 98308
  513.0 2.0 copy-start.8
  513.0 2.0 copy-start.18
Sparse Core Ops, SparseCore 0:
  515.2 276.3 all-reduce.2
where the time goes:
time: 810 us; the launch traced here: 800 us
  waiting for transfers between devices  412 us (51%)
  local copies, waits for them, and re-layouts  161 us (20%)
  other arithmetic  66.6 us (8%)
  starting transfers between devices  58.3 us (7%)
  matrix products  42.7 us (5%)
  loops' own time  39.3 us (5%)
  between operations  20.5 us (3%)
    unnamed x2, waiting for transfers between devices  275 us
    all_to_all x1, waiting for transfers between devices, local(): lax.all_to_all(solved, 'bulk', split_axis=0, concat_axis=2, tiled=True)  47.1 us
    unnamed x56, local copies, waits for them, and re-layouts  47 us
    all_to_all x1, waiting for transfers between devices, local(): lax.all_to_all(spatial_x, 'row', split_axis=1, concat_axis=3, tiled=True)  43.8 us
    another operation x8, loops' own time, apply_green(): lax.fori_loop(tile_shells[0], tile_shells[tile_width - 1] + 1, add_shell,...  39.3 us
    all_to_all x1, waiting for transfers between devices, local(): lax.all_to_all(spectrum, 'row', split_axis=3, concat_axis=1, tiled=True)  27.1 us
    all_to_all x1, starting transfers between devices, local(): lax.all_to_all(planes_k, 'bulk', split_axis=2, concat_axis=0, tiled=True)  23.4 us
    all_to_all x1, waiting for transfers between devices, local(): lax.all_to_all(planes_k, 'bulk', split_axis=2, concat_axis=0, tiled=True)  18.9 us
  transfers between devices with their start and end apart: 5, of which 5 were waited for; matrix products, arithmetic and copies ran while one was open for 5% of the time, Pallas kernels for 0%

commit v1 on v0

v1 whole, which is shorter than its diff:
```python
import math

import jax
import jax.numpy as jnp
import numpy as np
from jax import lax
from jax.sharding import PartitionSpec as P

mode = lax.Precision.HIGH


def owned_ky(rows, bulks):
    r = np.arange(rows)[:, None]
    b = np.arange(bulks)[None, :]
    return np.where(b < bulks // 2, 16 * b + r, 16 * (bulks - 1 - b) + 8 + r).reshape(-1)


def tables(n, rows, bulks):
    ky = owned_ky(rows, bulks)
    i = np.arange(n)
    turn = 2.0 * np.pi / n
    angle = turn * (ky[:, None] * i[None, :] % n)
    fwd = np.stack([np.cos(angle), -np.sin(angle)])
    inv = 2.0 * fwd
    zero = np.flatnonzero(ky == 0)[0]
    sign = np.where(i % 2 == 0, 1.0, -1.0)
    fwd[0, zero], fwd[1, zero] = 1.0, sign
    inv[0, zero], inv[1, zero] = 1.0, sign
    inv = inv / (n * n)
    angle = turn * (i[:, None] * i[None, :] % n)
    c, s = np.cos(angle), np.sin(angle)
    full = np.array([[c, -s], [s, c]])
    half = np.where(i[None, :] <= n // 2, c, s) * np.sqrt(2.0)
    half[:, 0], half[:, n // 2] = 1.0, sign
    none = np.zeros_like(half)
    packed = np.array([[half, none], [none, half]])
    both = []
    for m in (full, packed):
        m = m.transpose(0, 2, 1, 3).reshape(2, rows, n // rows, 2 * n)
        both.append(m.transpose(1, 0, 2, 3).reshape(2 * n, 2 * n))
    return fwd.astype(np.float32), inv.astype(np.float32), np.stack(both).astype(np.float32)


def local(charge, green, shells, planes):
    nxl, nzl, n = charge.shape
    rows, bulks = lax.axis_size("row"), lax.axis_size("bulk")
    r, b = lax.axis_index("row"), lax.axis_index("bulk")
    fwd, inv, mats = tables(n, rows, bulks)
    devices = rows * bulks
    axes = ("row", "bulk")
    own = jnp.where(b < bulks // 2, r, 8 - r)
    row_own = lax.dynamic_slice_in_dim(shells, own, 1, 0)
    row_far = lax.ppermute(shells[:1], "bulk", [(bulks // 2, 0)])
    first = (r == 0) & (b == 0)
    labels = jnp.concatenate([row_own, jnp.where(first, row_far, row_own)], axis=1)
    mat = lax.dynamic_index_in_dim(jnp.asarray(mats), first.astype(jnp.int32), 0, keepdims=False)

    sent = jnp.einsum("rdy,xzy->dzrx", fwd, charge, precision=mode).reshape(devices, nzl, 2 * nxl)
    got = lax.all_to_all(sent, axes, 0, 0, tiled=True)
    cols = got.reshape(rows, bulks * nzl, 2 * nxl).transpose(1, 0, 2).reshape(bulks * nzl, 2 * n)
    spec = jnp.dot(cols, mat, precision=mode)
    solved = jnp.zeros_like(spec)
    for s in range(green.shape[0]):
        solved = solved + jnp.dot(green[s], jnp.where(labels == s, spec, 0.0), precision=mode)
    back = lax.dot_general(solved, mat, (((1,), (1,)), ((), ())), precision=mode)
    picked = jnp.take(back, planes, axis=0).reshape(4, rows, 2, 8, 8)
    picked = picked.transpose(1, 0, 3, 2, 4).reshape(devices, 2, 8)
    back = back.reshape(bulks * nzl, rows, 2 * nxl).transpose(1, 0, 2).reshape(devices, nzl, 2 * nxl)
    home = lax.all_to_all(back, axes, 0, 0, tiled=True).reshape(devices, nzl, 2, nxl)
    field = jnp.einsum("dzrx,rdy->xzy", home, inv, precision=mode)
    part = lax.all_to_all(picked, axes, 0, 0, tiled=True)
    part = jnp.einsum("drx,rdy->xy", part, inv, precision=mode)
    part = part.reshape(8, bulks, n // bulks).transpose(1, 0, 2)
    part = lax.all_to_all(part, "bulk", 0, 0, tiled=True)
    return field, part.reshape(4, 8 * 8, n // bulks)


def solution(mesh):
    placed = (P("row", "bulk", None), P(), P("bulk", None), P())
    return jax.shard_map(
        local,
        mesh=mesh,
        in_specs=placed,
        out_specs=(P("row", "bulk", None), P(None, "row", "bulk")),
        check_vma=False,
    )
```

time: 810 us -> 146 us (0.18); the launches traced: 800 us -> 146 us
  waiting for transfers between devices: 412 us -> 66.7 us
  local copies, waits for them, and re-layouts: 161 us -> 8.57 us
  other arithmetic: 66.6 us -> 1.53 us
  loops' own time: 39.3 us -> 0 us
  starting transfers between devices: 58.3 us -> 27.1 us
  matrix products: 42.7 us -> 20.7 us
  blocking collectives: 0 us -> 20.4 us
  between operations: 20.5 us -> 0.97 us
    unnamed x2 -> x0, waiting for transfers between devices: 275 us -> none
    all_to_all x4 -> x3, waiting for transfers between devices: 137 us -> 66.7 us  [the longest x1 30.5 us: local(): lax.all_to_all(back, axes, 0, 0, tiled=True).reshape(devices, nzl, 2, nxl)]
    unnamed x56 -> x16, local copies, waits for them, and re-layouts: 47 us -> 3.13 us
    another operation x8 -> x0, loops' own time: 39.3 us -> none  [apply_green(): lax.fori_loop(tile_shells[0], tile_shells[tile_width - 1] + 1, add_shell,...]
    all_to_all x4 -> x3, starting transfers between devices: 58.2 us -> 26.3 us  [the longest x1 15.7 us: local(): got = lax.all_to_all(sent, axes, 0, 0, tiled=True)]
    all_to_all x4 -> x1, other arithmetic: 30.5 us -> 0.68 us  [local(): part = lax.all_to_all(part, 'bulk', 0, 0, tiled=True)]
    gather x3 -> x2, local copies, waits for them, and re-layouts: 28.9 us -> 0.73 us  [local(): picked = jnp.take(back, planes, axis=0).reshape(4, rows, 2, 8, 8)]
    all_to_all x7 -> x2, local copies, waits for them, and re-layouts: 27.6 us -> 0.9 us  [the longest x1 0.51 us: local(): part = lax.all_to_all(part, 'bulk', 0, 0, tiled=True)]
  transfers between devices with their start and end apart: 5 -> 4, of which waited for: 5 -> 3; matrix products, arithmetic and copies ran while one was open for 5% -> 3% of each run, Pallas kernels for 0% -> 0%
where the time goes in v1:
time: 146 us
  waiting for transfers between devices  66.7 us (46%)
  starting transfers between devices  27.1 us (19%)
  matrix products  20.7 us (14%)
  blocking collectives  20.4 us (14%)
  local copies, waits for them, and re-layouts  8.57 us (6%)
  other arithmetic  1.53 us (1%)
    all_to_all x1, waiting for transfers between devices, local(): lax.all_to_all(back, axes, 0, 0, tiled=True).reshape(devices, nzl, 2, nxl)  30.5 us
    all_to_all x1, waiting for transfers between devices, local(): got = lax.all_to_all(sent, axes, 0, 0, tiled=True)  30.1 us
    all_to_all x1, blocking collectives, local(): part = lax.all_to_all(picked, axes, 0, 0, tiled=True)  20.4 us
    all_to_all x1, starting transfers between devices, local(): got = lax.all_to_all(sent, axes, 0, 0, tiled=True)  15.7 us
    dot_general x8, matrix products, local(): jnp.dot(green[s], jnp.where(labels == s, spec, 0.0), precision=mode)  8.13 us
    all_to_all x1, starting transfers between devices, local(): lax.all_to_all(back, axes, 0, 0, tiled=True).reshape(devices, nzl, 2, nxl)  6.6 us
    all_to_all x1, waiting for transfers between devices, local(): part = lax.all_to_all(part, 'bulk', 0, 0, tiled=True)  6.07 us
    dot_general x1, matrix products, local(): spec = jnp.dot(cols, mat, precision=mode)  4.27 us
  transfers between devices with their start and end apart: 4, of which 3 were waited for; matrix products, arithmetic and copies ran while one was open for 3% of the time, Pallas kernels for 0%

profile of v1, /device:TPU:1, one launch (start us, length us, event | category | flops | bytes accessed | tf_op | source)
XLA Modules:
  0.0 145.9 jit_solution(3311211063886304750)
XLA Ops:
  0.6 3.0 %convolution_bitcast_fusion.1 = f32[256,8,2,64]{0,3,1,2:T(8,128)S(1)} fusion(f32[2,256,512,1]{2,1,3,0:T(8,128)} %constant.62, f32[64,8,512]{2,1,0:T(8,128)} %param.8), kind=kOutput, calls=%fused_computation.8 | convolution fusion | flops 805306368 | bytes 3145728 | tf_op jit(solution)/shard_map/rdy,xzy->dzrx/dot_general | solution.py:58
  3.6 0.1 copy.32
  3.7 0.0 copy-start.3
  3.7 1.3 copy.33
  5.0 15.7 %all-to-all-start = ((f32[256,8,128]{2,1,0:T(8,128)}), f32[256,8,128]{2,1,0:T(8,128)S(1)}, u32[]{:S(2)}, u32[]{:S(2)}) async-start(f32[256,8,128]{2,1,0:T(8,128)} %copy.33), calls=%async_computation | async-start | bytes 2097152 | tf_op jit(solution)/shard_map/all_to_all | solution.py:59
  20.7 0.7 slice.27
  21.4 0.8 collective-permute-start
  22.3 0.0 copy-done.3
  22.3 0.0 collective-permute-done
  22.3 0.7 broadcast_select_fusion
  23.1 30.1 %all-to-all-done = f32[256,8,128]{2,1,0:T(8,128)S(1)} async-done(((f32[256,8,128]{2,1,0:T(8,128)}), f32[256,8,128]{2,1,0:T(8,128)S(1)}, u32[]{:S(2)}, u32[]{:S(2)}) %all-to-all-start) | async-done | bytes 1048608 | tf_op jit(solution)/shard_map/all_to_all | solution.py:59
  53.2 0.3 copy.34
  53.5 0.0 copy-start
  53.5 4.3 %fusion.2 = f32[256,1024]{1,0:T(8,128)S(1)} fusion(f32[256,1024]{0,1:T(8,128)S(1)} %bitcast.75, f32[2,1024,1024]{2,1,0:T(8,128)} %constant.57.clone, s32[]{:T(128)S(6)} %select_n.58), kind=kOutput, calls=%fused_computation.3 | convolution fusion | flops 1610612736 | bytes 6291460 | tf_op jit(solution)/shard_map/dot_general | solution.py:61
  57.8 0.0 copy-done
  57.8 1.0 fusion.15
  58.9 1.0 convolution_add_fusion.6
  59.9 1.0 convolution_add_fusion.5
  60.9 0.0 slice-start
  60.9 1.0 convolution_add_fusion.4
  61.9 1.0 convolution_add_fusion.3
  63.0 0.0 slice-start.1
  63.0 1.0 convolution_add_fusion.2
  64.0 1.0 convolution_add_fusion.1
  65.0 1.0 convolution_add_fusion
  66.1 3.9 %fusion = f32[256,1024]{1,0:T(8,128)S(1)} fusion(f32[1024,256]{1,0:T(8,128)S(1)} %convolution_add_fusion, f32[2,1024,1024]{2,1,0:T(8,128)S(1)} %bitcast.73, s32[]{:T(128)S(6)} %select_n.58), kind=kOutput, calls=%fused_computation.1 | convolution fusion | flops 1610612736 | bytes 6291460 | tf_op jit(solution)/shard_map/dot_general | solution.py:65
  70.0 0.0 copy-start.2
  70.0 0.6 gather_fusion
  70.5 0.2 gather.7
  70.7 0.1 select_bitcast_fusion
  70.8 0.1 copy.37
  70.9 20.4 %all_to_all.20 = f32[256,2,8]{2,1,0:T(2,128)S(1)} all-to-all(f32[256,2,8]{2,1,0:T(2,128)S(1)} %bitcast.78), channel_id=1, replica_groups=mesh['bulk'=32,'row'=8] {'row','bulk'}, dimensions={0} | all-to-all | bytes 32768 | tf_op jit(solution)/shard_map/all_to_all | solution.py:71
  91.3 0.4 convolution_bitcast_fusion.2
  91.7 0.1 reshape.194
  91.9 0.1 copy.39
  91.9 0.7 reshape.210
  92.7 4.1 %all-to-all-start.3 = ((f32[32,1,128]{2,1,0:T(1,128)}), f32[32,1,128]{2,1,0:T(1,128)S(1)}, u32[]{:S(2)}, u32[]{:S(2)}) async-start(f32[32,1,128]{2,1,0:T(1,128)} %reshape.210), calls=%async_computation.3 | async-start | bytes 32768 | tf_op jit(solution)/shard_map/all_to_all | solution.py:74
  96.7 1.0 copy_bitcast_fusion
  97.8 6.1 %all-to-all-done.3 = f32[32,1,128]{2,1,0:T(1,128)S(1)} async-done(((f32[32,1,128]{2,1,0:T(1,128)}), f32[32,1,128]{2,1,0:T(1,128)S(1)}, u32[]{:S(2)}, u32[]{:S(2)}) %all-to-all-start.3) | async-done | bytes 16416 | tf_op jit(solution)/shard_map/all_to_all | solution.py:74
  103.8 6.6 %all-to-all-start.1 = ((f32[256,8,128]{2,1,0:T(8,128)}), f32[256,8,128]{2,1,0:T(8,128)S(1)}, u32[]{:S(2)}, u32[]{:S(2)}) async-start(f32[256,8,128]{2,1,0:T(8,128)} %bitcast.20), calls=%async_computation.1 | async-start | bytes 2097152 | tf_op jit(solution)/shard_map/all_to_all | solution.py:69
  110.4 0.5 broadcast.60
  111.0 0.7 reduce
  111.6 0.1 reshape.211
  111.7 0.7 copy.41
  112.4 30.5 %all-to-all-done.1 = f32[256,8,128]{2,1,0:T(8,128)S(1)} async-done(((f32[256,8,128]{2,1,0:T(8,128)}), f32[256,8,128]{2,1,0:T(8,128)S(1)}, u32[]{:S(2)}, u32[]{:S(2)}) %all-to-all-start.1) | async-done | bytes 1048608 | tf_op jit(solution)/shard_map/all_to_all | solution.py:69
  142.9 0.4 copy.36
  143.3 1.0 convolution_bitcast_fusion
  144.3 1.6 %copy.40 = f32[64,8,512]{2,1,0:T(8,128)} copy(f32[64,8,512]{2,0,1:T(8,128)S(1)} %convolution_bitcast_fusion) | data formatting | bytes 2097152
  (10 shorter events, 0.0 us)
Async XLA Ops:
  3.7 18.6 %copy-start.3 = (s32[4]{0:T(128)S(1)}, s32[4]{0:T(128)}, u32[]{:S(2)}) copy-start(s32[4]{0:T(128)} %param.11) | copy-start | bytes 52
  5.0 48.2 %all-to-all-start = ((f32[256,8,128]{2,1,0:T(8,128)}), f32[256,8,128]{2,1,0:T(8,128)S(1)}, u32[]{:S(2)}, u32[]{:S(2)}) async-start(f32[256,8,128]{2,1,0:T(8,128)} %copy.33), calls=%async_computation | async-start | bytes 2097152 | tf_op jit(solution)/shard_map/all_to_all | solution.py:59
  21.4 0.9 collective-permute-start
  53.5 4.3 %copy-start = (f32[8,256,256]{2,1,0:T(8,128)S(1)}, f32[8,256,256]{2,1,0:T(8,128)}, u32[]{:S(2)}) copy-start(f32[8,256,256]{2,1,0:T(8,128)} %param.9) | copy-start | bytes 6291460
  60.9 5.2 %slice-start = ((s8[8388608]{0:T(1024)(128)(4,1)}), s8[4194304]{0:T(1024)(128)(4,1)S(1)}, s32[]{:S(2)}) async-start(s8[8388608]{0:T(1024)(128)(4,1)} %bitcast.72), calls=%async_computation.4 | async-start | bytes 8388608
  63.0 3.1 %slice-start.1 = ((s8[8388608]{0:T(1024)(128)(4,1)}), s8[4194304]{0:T(1024)(128)(4,1)S(1)}, s32[]{:S(2)}) async-start(s8[8388608]{0:T(1024)(128)(4,1)} %bitcast.72), calls=%async_computation.5 | async-start | bytes 8388608
  70.0 21.4 %copy-start.2 = (f32[2,256,512]{2,1,0:T(8,128)S(1)}, f32[2,256,512]{2,1,0:T(8,128)}, u32[]{:S(2)}) copy-start(f32[2,256,512]{2,1,0:T(8,128)} %constant.59.clone) | copy-start | bytes 3145732
  92.7 11.2 %all-to-all-start.3 = ((f32[32,1,128]{2,1,0:T(1,128)}), f32[32,1,128]{2,1,0:T(1,128)S(1)}, u32[]{:S(2)}, u32[]{:S(2)}) async-start(f32[32,1,128]{2,1,0:T(1,128)} %reshape.210), calls=%async_computation.3 | async-start | bytes 32768 | tf_op jit(solution)/shard_map/all_to_all | solution.py:74
  103.8 39.5 %copy-start.1 = (f32[2,256,512,1]{2,1,0,3:T(8,128)S(1)}, f32[2,256,512,1]{2,1,0,3:T(8,128)}, u32[]{:S(2)}) copy-start(f32[2,256,512,1]{2,1,0,3:T(8,128)} %constant.63) | copy-start | bytes 3145732
  103.8 39.1 %all-to-all-start.1 = ((f32[256,8,128]{2,1,0:T(8,128)}), f32[256,8,128]{2,1,0:T(8,128)S(1)}, u32[]{:S(2)}, u32[]{:S(2)}) async-start(f32[256,8,128]{2,1,0:T(8,128)} %bitcast.20), calls=%async_computation.1 | async-start | bytes 2097152 | tf_op jit(solution)/shard_map/all_to_all | solution.py:69

commit v2 on v1

v2 whole, which is shorter than its diff:
```python
import functools

import jax
import jax.numpy as jnp
import ml_dtypes
import numpy as np
from jax import lax
from jax.experimental import pallas as pl
from jax.experimental.pallas import tpu as pltpu
from jax.sharding import PartitionSpec as P

MESH = pl.DeviceIdType.MESH
ROWS, BULKS = 8, 32
DEVICES = ROWS * BULKS
HALF = DEVICES // 2
N = 512
NZ = 256
HOT = 10


def owned_ky():
    r = np.arange(ROWS)[:, None]
    b = np.arange(BULKS)[None, :]
    return np.where(b < BULKS // 2, 16 * b + r, 16 * (BULKS - 1 - b) + 8 + r).reshape(-1)


def split_table(a):
    a = np.asarray(a, np.float64)
    hi = a.astype(np.float32).astype(ml_dtypes.bfloat16)
    lo = (a - hi.astype(np.float64)).astype(np.float32).astype(ml_dtypes.bfloat16)
    return np.stack([hi, lo])


def tables():
    n = N
    ky = owned_ky()
    i = np.arange(n)
    turn = 2.0 * np.pi / n
    angle = turn * (ky[:, None] * i[None, :] % n)
    fwd = np.stack([np.cos(angle), -np.sin(angle)])
    inv = 2.0 * fwd
    zero = np.flatnonzero(ky == 0)[0]
    sign = np.where(i % 2 == 0, 1.0, -1.0)
    fwd[0, zero], fwd[1, zero] = 1.0, sign
    inv[0, zero], inv[1, zero] = 1.0, sign
    inv = inv / (n * n)
    angle = turn * (i[:, None] * i[None, :] % n)
    c, s = np.cos(angle), np.sin(angle)
    full = np.array([[c, -s], [s, c]])
    half = np.where(i[None, :] <= n // 2, c, s) * np.sqrt(2.0)
    half[:, 0], half[:, n // 2] = 1.0, sign
    none = np.zeros_like(half)
    packed = np.array([[half, none], [none, half]])
    both = []
    for m in (full, packed):
        m = m.transpose(0, 2, 1, 3).reshape(2, ROWS, n // ROWS, 2 * n)
        both.append(m.transpose(1, 0, 2, 3).reshape(2 * n, 2 * n))
    both = np.stack(both)
    mats = split_table(both).transpose(1, 0, 2, 3)
    mats_t = split_table(both.transpose(0, 2, 1)).transpose(1, 0, 2, 3)
    fwd = split_table(fwd.reshape(2 * DEVICES, n))
    inv_t = split_table(inv.transpose(0, 2, 1).reshape(2 * n, DEVICES))
    inv = split_table(inv.reshape(2 * DEVICES, n))
    return fwd, mats, mats_t, inv, inv_t


def parts(x):
    hi = x.astype(jnp.bfloat16)
    lo = (x - hi.astype(jnp.float32)).astype(jnp.bfloat16)
    return hi, lo


def dot(a, b, dims=((1,), (0,))):
    return lax.dot_general(a, b, (dims, ((), ())), preferred_element_type=jnp.float32)


def dot3(ah, al, bh, bl, dims=((1,), (0,))):
    return dot(ah, bh, dims) + dot(ah, bl, dims) + dot(al, bh, dims)


def kernel(
    charge, fwd, shells, planes, green, mats, mats_t, inv, inv_t,
    out, electrodes,
    sbuf, rbuf, obuf, home, mat, mat_t, inv_v, inv_t_v, g32, g_hi, g_lo, x_hi, x_lo, v_hi, v_lo,
    lab, lab_src, lab_far, ebuf, erecv, eout, elrecv,
    table_sem, ssem, rsem, hssem, hrsem, essem, ersem, elssem, elrsem, lssem, lrsem,
):
    r, b = lax.axis_index("row"), lax.axis_index("bulk")
    m = r * BULKS + b
    core = lax.rem(b, 2)
    first = m == 0
    feeder = m == BULKS // 2
    hot = lax.rem(b, HOT) == 0

    def at(d):
        return {"row": lax.div(d, BULKS), "bulk": lax.rem(d, BULKS)}

    def tile(ref, d):
        return ref.at[pl.ds(pl.multiple_of(d * 8, 8), 8), :]

    def push(src, dst, d, ss, rs):
        return pltpu.make_async_remote_copy(
            src_ref=src, dst_ref=dst, send_sem=ss, recv_sem=rs, device_id=at(d), device_id_type=MESH
        )

    def drain(ref, sem):
        pltpu.make_async_copy(ref, ref, sem).wait()

    barrier = pltpu.get_barrier_semaphore()

    def greet(i, c):
        pl.semaphore_signal(barrier, inc=1, device_id=at(lax.rem(m + i, DEVICES)), device_id_type=MESH)
        return c

    lax.fori_loop(1, DEVICES, greet, 0)

    which = jnp.where(first, 1, 0)
    loads = [
        pltpu.make_async_copy(src, dst, table_sem.at[i])
        for i, (src, dst) in enumerate(
            [(green, g32), (mats.at[which], mat), (mats_t.at[which], mat_t), (inv, inv_v), (inv_t, inv_t_v)]
        )
    ]
    for load in loads:
        load.start()

    lane = lax.broadcasted_iota(jnp.int32, (DEVICES, 128), 1)
    for q in range(2):
        rows = jnp.concatenate([charge[:, 4 * q + j, :] for j in range(4)], axis=0)
        c_hi, c_lo = parts(rows)
        spec = dot3(fwd[0], fwd[1], c_hi, c_lo, ((1,), (1,)))
        for p in range(2):
            re = spec[:DEVICES, 128 * p : 128 * (p + 1)]
            im = spec[DEVICES:, 128 * p : 128 * (p + 1)]
            z = 4 * q + 2 * p
            sbuf[pl.ds(z, DEVICES, stride=8), :] = jnp.where(lane < 64, re, pltpu.roll(im, 64, 1))
            sbuf[pl.ds(z + 1, DEVICES, stride=8), :] = jnp.where(lane < 64, pltpu.roll(re, 64, 1), im)

    own = shells[pl.ds(jnp.where(b < BULKS // 2, r, 8 - r), 1), :]
    lab[:, :N] = own
    lab_src[...] = shells[0:1, :]

    pl.semaphore_wait(barrier, DEVICES - 1)

    keep = pltpu.make_async_copy(tile(sbuf, m), tile(rbuf, m), rsem)
    keep.start()
    pair = lax.div(m, 2)
    for c in range(2):

        @pl.when(core != c)
        def _(c=c):
            d = 2 * pair + c
            push(tile(sbuf, d), tile(rbuf, m), d, ssem, rsem).start()

        def send(j, carry, c=c):
            d = 2 * lax.rem(pair + j, HALF) + c
            push(tile(sbuf, d), tile(rbuf, m), d, ssem, rsem).start()
            return carry

        lax.fori_loop(1, HALF, send, 0)

    @pl.when(feeder)
    def _():
        push(lab_src, lab_far, 0, lssem, lrsem).start()

    loads[0].wait()
    for s in range(8):
        hi, lo = parts(g32[s])
        g_hi[s] = hi
        g_lo[s] = lo
    loads[1].wait()
    loads[2].wait()

    @pl.when(feeder)
    def _():
        drain(lab_src, lssem)

    @pl.when(first)
    def _():
        drain(lab_far, lrsem)
        lab[:, N:] = lab_far[...]

    @pl.when(jnp.logical_not(first))
    def _():
        lab[:, N:] = lab[:, :N]

    drain(rbuf, rsem)

    for k in range(ROWS):
        hi, lo = parts(rbuf[pl.ds(k * NZ, NZ), :])
        x_hi[:, k * 128 : (k + 1) * 128] = hi
        x_lo[:, k * 128 : (k + 1) * 128] = lo

    def solve(t, carry):
        cols = pl.ds(pl.multiple_of(t * 256, 256), 256)
        spec = dot3(x_hi[...], x_lo[...], mat[0, :, cols], mat[1, :, cols])
        s_hi, s_lo = parts(spec)
        label = lab[:, cols]

        acc = jnp.zeros((NZ, 256), jnp.float32)
        for s in range(8):
            mask = label == s
            m_hi = jnp.where(mask, s_hi, jnp.zeros_like(s_hi))
            m_lo = jnp.where(mask, s_lo, jnp.zeros_like(s_lo))
            acc = acc + dot3(g_hi[s], g_lo[s], m_hi, m_lo)
        hi, lo = parts(acc)
        v_hi[:, cols] = hi
        v_lo[:, cols] = lo
        return carry

    lax.fori_loop(0, 4, solve, 0)

    hkeep = pltpu.make_async_copy(tile(obuf, m), tile(home, m), hrsem)
    y = lax.div(r, 2)

    def give(t, carry):
        g = lax.rem(y + t, 4)
        cols = pl.ds(pl.multiple_of(g * 256, 256), 256)
        back = dot3(v_hi[...], v_lo[...], mat_t[0, :, cols], mat_t[1, :, cols])
        for h in range(2):
            obuf[pl.ds(pl.multiple_of((2 * g + h) * NZ, NZ), NZ), :] = back[:, h * 128 : (h + 1) * 128]
        for h in range(2):
            for p in range(4):
                k = (2 * g + h) * 4 + p
                ebuf[k] = obuf[pl.ds((2 * g + h) * NZ + planes[p], 1), :]
                d = (2 * g + h) * BULKS + HOT * p

                @pl.when(d != m)
                def _():
                    push(ebuf.at[k], erecv.at[m], d, essem, ersem).start()

                @pl.when(d == m)
                def _():
                    pltpu.make_async_copy(ebuf.at[k], erecv.at[m], ersem).start()

        @pl.when(t == 0)
        def _():
            hkeep.start()

        base = lax.rem(m, 64)

        def send(j, c):
            d = g * 64 + lax.rem(base + j, 64)
            push(tile(obuf, d), tile(home, m), d, hssem, hrsem).start()
            return c

        lax.fori_loop(jnp.where(t == 0, 1, 0), 64, send, 0)
        return carry

    lax.fori_loop(0, 4, give, 0)
    loads[3].wait()
    loads[4].wait()

    @pl.when(hot)
    def _():
        drain(erecv, ersem)
        e_hi, e_lo = parts(erecv[...].reshape(DEVICES, 128))
        both = dot3(inv_t_v[0], inv_t_v[1], e_hi, e_lo)
        eout[...] = both[:N] + pltpu.roll(both[N:], 64, 1)
        p = lax.div(b, HOT)

        def spread(j, c):
            d = r * BULKS + lax.rem(b + j, BULKS)
            src = eout.at[pl.ds(pl.multiple_of(lax.rem(d, BULKS) * 16, 16), 16), :]
            push(src, elrecv.at[p], d, elssem, elrsem).start()
            return c

        pltpu.make_async_copy(eout.at[pl.ds(pl.multiple_of(b * 16, 16), 16), :], elrecv.at[p], elrsem).start()
        lax.fori_loop(1, BULKS, spread, 0)

    drain(home, hrsem)
    for q in range(2):
        re, im = [], []
        for j in range(4):
            flip = jnp.transpose(home[pl.ds(4 * q + j, DEVICES, stride=8), :])
            re.append(flip[:64])
            im.append(flip[64:])
        w_hi, w_lo = parts(jnp.concatenate([jnp.concatenate(re, axis=0), jnp.concatenate(im, axis=0)], axis=1))
        field = dot3(w_hi, w_lo, inv_v[0], inv_v[1])
        for j in range(4):
            out[:, 4 * q + j, :] = field[64 * j : 64 * (j + 1)]

    drain(elrecv, elrsem)
    for p in range(4):
        electrodes[p] = jnp.transpose(elrecv[p])[:64, :]

    drain(sbuf.at[pl.ds(0, 8 * (DEVICES - 1)), :], ssem)
    drain(obuf.at[pl.ds(0, 8 * (DEVICES - 1)), :], hssem)
    drain(ebuf.at[pl.ds(0, 31)], essem)

    @pl.when(jnp.logical_not(hot))
    def _():
        drain(ebuf.at[0], essem)

    @pl.when(hot)
    def _():
        drain(eout.at[pl.ds(0, 16 * (BULKS - 1)), :], elssem)


def local(charge, green, shells, planes):
    fwd, mats, mats_t, inv, inv_t = (jnp.asarray(t) for t in tables())
    f32, bf16 = jnp.float32, jnp.bfloat16
    vmem, hbm = pl.BlockSpec(memory_space=pltpu.VMEM), pl.BlockSpec(memory_space=pl.ANY)
    dma = pltpu.SemaphoreType.DMA
    return pl.pallas_call(
        kernel,
        out_shape=(
            jax.ShapeDtypeStruct(charge.shape, f32),
            jax.ShapeDtypeStruct((4, N // ROWS, N // BULKS), f32),
        ),
        in_specs=[vmem, vmem, vmem, pl.BlockSpec(memory_space=pltpu.SMEM), hbm, hbm, hbm, hbm, hbm],
        out_specs=(vmem, vmem),
        scratch_shapes=[
            pltpu.VMEM((8 * DEVICES, 128), f32),
            pltpu.VMEM((8 * DEVICES, 128), f32),
            pltpu.VMEM((8 * DEVICES, 128), f32),
            pltpu.VMEM((8 * DEVICES, 128), f32),
            pltpu.VMEM((2, 2 * N, 2 * N), bf16),
            pltpu.VMEM((2, 2 * N, 2 * N), bf16),
            pltpu.VMEM((2, 2 * DEVICES, N), bf16),
            pltpu.VMEM((2, 2 * N, DEVICES), bf16),
            pltpu.VMEM((8, NZ, NZ), f32),
            pltpu.VMEM((8, NZ, NZ), bf16),
            pltpu.VMEM((8, NZ, NZ), bf16),
            pltpu.VMEM((NZ, 2 * N), bf16),
            pltpu.VMEM((NZ, 2 * N), bf16),
            pltpu.VMEM((NZ, 2 * N), bf16),
            pltpu.VMEM((NZ, 2 * N), bf16),
            pltpu.VMEM((1, 2 * N), jnp.int32),
            pltpu.VMEM((1, N), jnp.int32),
            pltpu.VMEM((1, N), jnp.int32),
            pltpu.VMEM((32, 1, 128), f32),
            pltpu.VMEM((DEVICES, 1, 128), f32),
            pltpu.VMEM((N, 128), f32),
            pltpu.VMEM((4, 16, 128), f32),
            dma((5,)),
        ]
        + [dma] * 10,
        compiler_params=pltpu.CompilerParams(
            collective_id=0, has_side_effects=True, vmem_limit_bytes=48 * 1024 * 1024
        ),
    )(charge, fwd, shells, planes, green, mats, mats_t, inv, inv_t)


def solution(mesh):
    placed = (P("row", "bulk", None), P(), P("bulk", None), P())
    return jax.shard_map(
        local,
        mesh=mesh,
        in_specs=placed,
        out_specs=(P("row", "bulk", None), P(None, "row", "bulk")),
        check_vma=False,
    )
```

time: 146 us -> 85 us (0.58)
  Pallas kernels: 0 us -> 76.1 us
  waiting for transfers between devices: 66.7 us -> 0 us
  starting transfers between devices: 27.1 us -> 0 us
  matrix products: 20.7 us -> 0 us
  blocking collectives: 20.4 us -> 0 us
  other arithmetic: 1.53 us -> 0 us
    pallas_call x0 -> x1, Pallas kernels: none -> 76.1 us  [local(): pl.pallas_call(kernel, out_shape=(jax.ShapeDtypeStruct(charge.shape, f32)...]
    all_to_all x3 -> x0, waiting for transfers between devices: 66.7 us -> none  [the longest x1 30.5 us: local(): lax.all_to_all(back, axes, 0, 0, tiled=True).reshape(devices, nzl, 2, nxl)]
    all_to_all x3 -> x0, starting transfers between devices: 26.3 us -> none  [the longest x1 15.7 us: local(): got = lax.all_to_all(sent, axes, 0, 0, tiled=True)]
    dot_general x13 -> x0, matrix products: 20.7 us -> none  [the longest x8 8.13 us: local(): jnp.dot(green[s], jnp.where(labels == s, spec, 0.0), precision=mode)]
    all_to_all x1 -> x0, blocking collectives: 20.4 us -> none  [local(): part = lax.all_to_all(picked, axes, 0, 0, tiled=True)]
    unnamed x16 -> x13, local copies, waits for them, and re-layouts: 3.13 us -> 7.27 us
    reshape x3 -> x0, local copies, waits for them, and re-layouts: 2.45 us -> none  [the longest x1 1.31 us: local(): jnp.einsum('rdy,xzy->dzrx', fwd, charge, precision=mode)]
  transfers between devices with their start and end apart: 4 -> 0, of which waited for: 3 -> 0; matrix products, arithmetic and copies ran while one was open for 3% -> 0% of each run, Pallas kernels for 0% -> 0%
where the time goes in v2:
time: 85 us; the launch traced here: 84.7 us
  Pallas kernels  76.1 us (90%)
  local copies, waits for them, and re-layouts  7.98 us (9%)
    pallas_call x1, Pallas kernels, local(): pl.pallas_call(kernel, out_shape=(jax.ShapeDtypeStruct(charge.shape, f32)...  76.1 us
    unnamed x13, local copies, waits for them, and re-layouts  7.27 us

profile of v2, /device:TPU:1, one launch (start us, length us, event | category | flops | bytes accessed | tf_op | source)
XLA Modules:
  0.0 84.7 jit_solution(482917270942777030)
XLA Ops:
  0.6 0.0 copy-start
  0.6 1.2 %copy-done = f32[64,8,512]{2,1,0:T(8,128)S(1)} copy-done((f32[64,8,512]{2,1,0:T(8,128)S(1)}, f32[64,8,512]{2,1,0:T(8,128)}, u32[]{:S(2)}) %copy-start) | copy-done | bytes 1048600
  1.9 0.0 copy-start.1
  1.9 1.2 %copy-done.1 = bf16[2,1024,256]{2,1,0:T(8,128)(2,1)S(1)} copy-done((bf16[2,1024,256]{2,1,0:T(8,128)(2,1)S(1)}, bf16[2,1024,256]{2,1,0:T(8,128)(2,1)}, u32[]{:S(2)}) %copy-start.1) | copy-done | bytes 1048600
  3.1 0.0 copy-start.2
  3.1 1.2 %copy-done.2 = bf16[2,512,512]{2,1,0:T(8,128)(2,1)S(1)} copy-done((bf16[2,512,512]{2,1,0:T(8,128)(2,1)S(1)}, bf16[2,512,512]{2,1,0:T(8,128)(2,1)}, u32[]{:S(2)}) %copy-start.2) | copy-done | bytes 1048600
  4.3 0.0 copy-start.3
  4.3 1.2 %copy-done.3 = bf16[2,512,512]{2,1,0:T(8,128)(2,1)S(1)} copy-done((bf16[2,512,512]{2,1,0:T(8,128)(2,1)S(1)}, bf16[2,512,512]{2,1,0:T(8,128)(2,1)}, u32[]{:S(2)}) %copy-start.3) | copy-done | bytes 1048600
  5.5 0.0 copy-start.4
  5.5 0.8 copy-done.4
  6.3 0.0 copy-start.5
  6.3 0.7 copy-done.5
  6.9 76.1 %shard_map.104 = (f32[64,8,512]{2,1,0:T(8,128)S(1)}, f32[4,64,16]{2,1,0:T(8,128)S(1)}) custom-call(f32[64,8,512]{2,1,0:T(8,128)S(1)} %copy-done, bf16[2,512,512]{2,1,0:T(8,128)(2,1)S(1)} %copy-done.3, s32[16,512]{1,0:T(8,128)S(1)} %copy-done.4, s32[4]{0:T(128)S(1)} %copy-done.5, f32[8,256,256]{2,1,0:T(8,128)} %green.1, ...), custom_call_target="tpu_custom_call" | custom-call | tf_op jit(solution)/shard_map/pallas_call | solution.py:305
  83.0 0.7 copy.11
  83.7 1.0 %copy.13 = f32[64,8,512]{2,1,0:T(8,128)} copy(f32[64,8,512]{2,1,0:T(8,128)S(1)} %get-tuple-element.6) | data formatting | bytes 2097152
Async XLA Ops:
  0.6 1.2 %copy-start = (f32[64,8,512]{2,1,0:T(8,128)S(1)}, f32[64,8,512]{2,1,0:T(8,128)}, u32[]{:S(2)}) copy-start(f32[64,8,512]{2,1,0:T(8,128)} %charge.1) | copy-start | bytes 3145732
  1.9 1.2 %copy-start.1 = (bf16[2,1024,256]{2,1,0:T(8,128)(2,1)S(1)}, bf16[2,1024,256]{2,1,0:T(8,128)(2,1)}, u32[]{:S(2)}) copy-start(bf16[2,1024,256]{2,1,0:T(8,128)(2,1)} %constant.14.clone.inv_t) | copy-start | bytes 3145732
  3.1 1.2 %copy-start.2 = (bf16[2,512,512]{2,1,0:T(8,128)(2,1)S(1)}, bf16[2,512,512]{2,1,0:T(8,128)(2,1)}, u32[]{:S(2)}) copy-start(bf16[2,512,512]{2,1,0:T(8,128)(2,1)} %constant.13.clone.inv) | copy-start | bytes 3145732
  4.3 1.2 %copy-start.3 = (bf16[2,512,512]{2,1,0:T(8,128)(2,1)S(1)}, bf16[2,512,512]{2,1,0:T(8,128)(2,1)}, u32[]{:S(2)}) copy-start(bf16[2,512,512]{2,1,0:T(8,128)(2,1)} %constant.10.clone.fwd) | copy-start | bytes 3145732
  5.5 0.8 copy-start.4
  6.3 0.7 copy-start.5

commit v3 on v2

--- a/solution.py
+++ b/solution.py
@@ -60,7 +60,7 @@
     mats_t = split_table(both.transpose(0, 2, 1)).transpose(1, 0, 2, 3)
     fwd = split_table(fwd.reshape(2 * DEVICES, n))
     inv_t = split_table(inv.transpose(0, 2, 1).reshape(2 * n, DEVICES))
-    inv = split_table(inv.reshape(2 * DEVICES, n))
+    inv = split_table(inv.reshape(2, HALF, 2, n).transpose(2, 0, 1, 3).reshape(2, DEVICES, n))
     return fwd, mats, mats_t, inv, inv_t
 
 
@@ -79,15 +79,18 @@
 
 
 def kernel(
-    charge, fwd, shells, planes, green, mats, mats_t, inv, inv_t,
+    charge_h, fwd_h, shells_h, planes_h, green, mats, mats_t, inv, inv_t,
     out, electrodes,
-    sbuf, rbuf, obuf, home, mat, mat_t, inv_v, inv_t_v, g32, g_hi, g_lo, x_hi, x_lo, v_hi, v_lo,
+    charge, fwd, shells, planes,
+    sbuf, rbuf, obuf, home, mat, mat_t, inv_v, inv_t_v, g32, g_hi, g_lo, spec_ref, v_hi, v_lo, field_ref,
     lab, lab_src, lab_far, ebuf, erecv, eout, elrecv,
-    table_sem, ssem, rsem, hssem, hrsem, essem, ersem, elssem, elrsem, lssem, lrsem,
+    gate, table_sem, ssem, rsem, hssem, hrsem, essem, ersem, elssem, elrsem, lssem, lrsem,
 ):
     r, b = lax.axis_index("row"), lax.axis_index("bulk")
     m = r * BULKS + b
     core = lax.rem(b, 2)
+    pair = lax.div(m, 2)
+    y, q0 = lax.div(pair, 32), lax.rem(pair, 32)
     first = m == 0
     feeder = m == BULKS // 2
     hot = lax.rem(b, HOT) == 0
@@ -106,24 +109,31 @@
     def drain(ref, sem):
         pltpu.make_async_copy(ref, ref, sem).wait()
 
+    which = jnp.where(first, 1, 0)
+    moves = [
+        (charge_h, charge), (fwd_h, fwd), (shells_h, shells), (planes_h, planes), (green, g32),
+        (mats.at[which], mat), (mats_t.at[which], mat_t), (inv, inv_v), (inv_t, inv_t_v),
+    ]
+    loads = [pltpu.make_async_copy(src, dst, table_sem.at[i]) for i, (src, dst) in enumerate(moves)]
+    for load in loads[:4]:
+        load.start()
+
     barrier = pltpu.get_barrier_semaphore()
-
-    def greet(i, c):
-        pl.semaphore_signal(barrier, inc=1, device_id=at(lax.rem(m + i, DEVICES)), device_id_type=MESH)
-        return c
-
-    lax.fori_loop(1, DEVICES, greet, 0)
-
-    which = jnp.where(first, 1, 0)
-    loads = [
-        pltpu.make_async_copy(src, dst, table_sem.at[i])
-        for i, (src, dst) in enumerate(
-            [(green, g32), (mats.at[which], mat), (mats_t.at[which], mat_t), (inv, inv_v), (inv_t, inv_t_v)]
-        )
-    ]
-    for load in loads:
+    z = lax.rem(r, 2) * 4 + lax.rem(lax.div(b, 2), 4)
+    x = lax.div(b, 8)
+
+    def place(px, py, pz, pc):
+        return {"row": py * 2 + lax.div(pz, 4), "bulk": px * 8 + lax.rem(pz, 4) * 2 + pc}
+
+    plane_peers = [place(lax.rem(x + i, 4), lax.rem(y + j, 4), z, core) for i in range(4) for j in range(4) if i + j]
+    line_peers = [place(x, y, lax.rem(z + i, 8), lax.rem(core + j, 2)) for i in range(8) for j in range(2) if i + j]
+    for peer in plane_peers + line_peers:
+        pl.semaphore_signal(barrier, inc=1, device_id=peer, device_id_type=MESH)
+    for load in loads[4:]:
         load.start()
 
+    loads[0].wait()
+    loads[1].wait()
     lane = lax.broadcasted_iota(jnp.int32, (DEVICES, 128), 1)
     for q in range(2):
         rows = jnp.concatenate([charge[:, 4 * q + j, :] for j in range(4)], axis=0)
@@ -132,29 +142,32 @@
         for p in range(2):
             re = spec[:DEVICES, 128 * p : 128 * (p + 1)]
             im = spec[DEVICES:, 128 * p : 128 * (p + 1)]
-            z = 4 * q + 2 * p
-            sbuf[pl.ds(z, DEVICES, stride=8), :] = jnp.where(lane < 64, re, pltpu.roll(im, 64, 1))
-            sbuf[pl.ds(z + 1, DEVICES, stride=8), :] = jnp.where(lane < 64, pltpu.roll(re, 64, 1), im)
-
-    own = shells[pl.ds(jnp.where(b < BULKS // 2, r, 8 - r), 1), :]
-    lab[:, :N] = own
+            k = 4 * q + 2 * p
+            sbuf[pl.ds(k, DEVICES, stride=8), :] = jnp.where(lane < 64, re, pltpu.roll(im, 64, 1))
+            sbuf[pl.ds(k + 1, DEVICES, stride=8), :] = jnp.where(lane < 64, pltpu.roll(re, 64, 1), im)
+
+    loads[2].wait()
+    loads[3].wait()
+    lab[:, :N] = shells[pl.ds(jnp.where(b < BULKS // 2, r, 8 - r), 1), :]
     lab_src[...] = shells[0:1, :]
 
-    pl.semaphore_wait(barrier, DEVICES - 1)
-
-    keep = pltpu.make_async_copy(tile(sbuf, m), tile(rbuf, m), rsem)
-    keep.start()
-    pair = lax.div(m, 2)
+    pl.semaphore_wait(barrier, len(plane_peers) + len(line_peers))
+    for peer in line_peers:
+        pl.semaphore_signal(gate, inc=1, device_id=peer, device_id_type=MESH)
+    pl.semaphore_wait(gate, len(line_peers))
+
+    pltpu.make_async_copy(tile(sbuf, m), tile(rbuf, m), rsem.at[y]).start()
     for c in range(2):
 
         @pl.when(core != c)
         def _(c=c):
             d = 2 * pair + c
-            push(tile(sbuf, d), tile(rbuf, m), d, ssem, rsem).start()
-
-        def send(j, carry, c=c):
-            d = 2 * lax.rem(pair + j, HALF) + c
-            push(tile(sbuf, d), tile(rbuf, m), d, ssem, rsem).start()
+            push(tile(sbuf, d), tile(rbuf, m), d, ssem, rsem.at[y]).start()
+
+        def send(i, carry, c=c):
+            t, j = lax.div(i, 32), lax.rem(i, 32)
+            d = 2 * (lax.rem(y + t, 4) * 32 + lax.rem(q0 + j, 32)) + c
+            push(tile(sbuf, d), tile(rbuf, m), d, ssem, rsem.at[y]).start()
             return carry
 
         lax.fori_loop(1, HALF, send, 0)
@@ -163,13 +176,13 @@
     def _():
         push(lab_src, lab_far, 0, lssem, lrsem).start()
 
-    loads[0].wait()
+    loads[4].wait()
     for s in range(8):
         hi, lo = parts(g32[s])
         g_hi[s] = hi
         g_lo[s] = lo
-    loads[1].wait()
-    loads[2].wait()
+    loads[5].wait()
+    loads[6].wait()
 
     @pl.when(feeder)
     def _():
@@ -184,19 +197,23 @@
     def _():
         lab[:, N:] = lab[:, :N]
 
-    drain(rbuf, rsem)
-
-    for k in range(ROWS):
-        hi, lo = parts(rbuf[pl.ds(k * NZ, NZ), :])
-        x_hi[:, k * 128 : (k + 1) * 128] = hi
-        x_lo[:, k * 128 : (k + 1) * 128] = lo
+    spec_ref[...] = jnp.zeros_like(spec_ref)
+
+    def gather(t, carry):
+        g = lax.rem(y + 4 - t, 4)
+        drain(rbuf.at[pl.ds(pl.multiple_of(g * 512, 512), 512), :], rsem.at[g])
+        rows = [rbuf[pl.ds(pl.multiple_of(g * 512 + h * NZ, NZ), NZ), :] for h in range(2)]
+        hi, lo = parts(jnp.concatenate(rows, axis=1))
+        deep = pl.ds(pl.multiple_of(g * 256, 256), 256)
+        spec_ref[...] += dot3(hi, lo, mat[0, deep, :], mat[1, deep, :])
+        return carry
+
+    lax.fori_loop(0, 4, gather, 0)
 
     def solve(t, carry):
         cols = pl.ds(pl.multiple_of(t * 256, 256), 256)
-        spec = dot3(x_hi[...], x_lo[...], mat[0, :, cols], mat[1, :, cols])
-        s_hi, s_lo = parts(spec)
+        s_hi, s_lo = parts(spec_ref[:, cols])
         label = lab[:, cols]
-
         acc = jnp.zeros((NZ, 256), jnp.float32)
         for s in range(8):
             mask = label == s
@@ -210,8 +227,7 @@
 
     lax.fori_loop(0, 4, solve, 0)
 
-    hkeep = pltpu.make_async_copy(tile(obuf, m), tile(home, m), hrsem)
-    y = lax.div(r, 2)
+    spot = core * HALF + pair
 
     def give(t, carry):
         g = lax.rem(y + t, 4)
@@ -235,21 +251,34 @@
 
         @pl.when(t == 0)
         def _():
-            hkeep.start()
-
-        base = lax.rem(m, 64)
+            pltpu.make_async_copy(tile(obuf, m), tile(home, spot), hrsem.at[core]).start()
+            d = m + 1 - 2 * core
+            push(tile(obuf, d), tile(home, spot), d, hssem, hrsem.at[core]).start()
 
         def send(j, c):
-            d = g * 64 + lax.rem(base + j, 64)
-            push(tile(obuf, d), tile(home, m), d, hssem, hrsem).start()
+            d = 2 * (g * 32 + lax.rem(q0 + j, 32))
+            push(tile(obuf, d), tile(home, spot), d, hssem, hrsem.at[core]).start()
+            push(tile(obuf, d + 1), tile(home, spot), d + 1, hssem, hrsem.at[core]).start()
             return c
 
-        lax.fori_loop(jnp.where(t == 0, 1, 0), 64, send, 0)
+        lax.fori_loop(jnp.where(t == 0, 1, 0), 32, send, 0)
         return carry
 
     lax.fori_loop(0, 4, give, 0)
-    loads[3].wait()
-    loads[4].wait()
+    loads[7].wait()
+    loads[8].wait()
+
+    def regain(c):
+        drain(home.at[pl.ds(c * 8 * HALF, 8 * HALF), :], hrsem.at[c])
+        re, im = [], []
+        for k in range(8):
+            flip = jnp.transpose(home[pl.ds(c * 8 * HALF + k, HALF, stride=8), :])
+            re.append(flip[:64])
+            im.append(flip[64:])
+        w_hi, w_lo = parts(jnp.concatenate([jnp.concatenate(re, axis=0), jnp.concatenate(im, axis=0)], axis=1))
+        return dot3(w_hi, w_lo, inv_v[0, c], inv_v[1, c])
+
+    field_ref[...] = regain(0)
 
     @pl.when(hot)
     def _():
@@ -268,21 +297,12 @@
         pltpu.make_async_copy(eout.at[pl.ds(pl.multiple_of(b * 16, 16), 16), :], elrecv.at[p], elrsem).start()
         lax.fori_loop(1, BULKS, spread, 0)
 
-    drain(home, hrsem)
-    for q in range(2):
-        re, im = [], []
-        for j in range(4):
-            flip = jnp.transpose(home[pl.ds(4 * q + j, DEVICES, stride=8), :])
-            re.append(flip[:64])
-            im.append(flip[64:])
-        w_hi, w_lo = parts(jnp.concatenate([jnp.concatenate(re, axis=0), jnp.concatenate(im, axis=0)], axis=1))
-        field = dot3(w_hi, w_lo, inv_v[0], inv_v[1])
-        for j in range(4):
-            out[:, 4 * q + j, :] = field[64 * j : 64 * (j + 1)]
+    rest = regain(1)
+    for k in range(8):
+        out[:, k, :] = field_ref[64 * k : 64 * (k + 1), :] + rest[64 * k : 64 * (k + 1)]
 
     drain(elrecv, elrsem)
-    for p in range(4):
-        electrodes[p] = jnp.transpose(elrecv[p])[:64, :]
+    electrodes[...] = elrecv[:, :, :64]
 
     drain(sbuf.at[pl.ds(0, 8 * (DEVICES - 1)), :], ssem)
     drain(obuf.at[pl.ds(0, 8 * (DEVICES - 1)), :], hssem)
@@ -299,47 +319,57 @@
 
 def local(charge, green, shells, planes):
     fwd, mats, mats_t, inv, inv_t = (jnp.asarray(t) for t in tables())
-    f32, bf16 = jnp.float32, jnp.bfloat16
-    vmem, hbm = pl.BlockSpec(memory_space=pltpu.VMEM), pl.BlockSpec(memory_space=pl.ANY)
+    f32, bf16, i32 = jnp.float32, jnp.bfloat16, jnp.int32
+    vmem, hbm = pl.BlockSpec(memory_space=pltpu.VMEM), pl.BlockSpec(memory_space=pltpu.HBM)
     dma = pltpu.SemaphoreType.DMA
-    return pl.pallas_call(
+    field, plates = pl.pallas_call(
         kernel,
         out_shape=(
             jax.ShapeDtypeStruct(charge.shape, f32),
-            jax.ShapeDtypeStruct((4, N // ROWS, N // BULKS), f32),
+            jax.ShapeDtypeStruct((4, N // BULKS, N // ROWS), f32),
         ),
-        in_specs=[vmem, vmem, vmem, pl.BlockSpec(memory_space=pltpu.SMEM), hbm, hbm, hbm, hbm, hbm],
+        in_specs=[hbm] * 9,
         out_specs=(vmem, vmem),
         scratch_shapes=[
+            pltpu.VMEM(charge.shape, f32),
+            pltpu.VMEM(fwd.shape, bf16),
+            pltpu.VMEM(shells.shape, i32),
+            pltpu.SMEM(planes.shape, i32),
             pltpu.VMEM((8 * DEVICES, 128), f32),
             pltpu.VMEM((8 * DEVICES, 128), f32),
             pltpu.VMEM((8 * DEVICES, 128), f32),
             pltpu.VMEM((8 * DEVICES, 128), f32),
-            pltpu.VMEM((2, 2 * N, 2 * N), bf16),
-            pltpu.VMEM((2, 2 * N, 2 * N), bf16),
-            pltpu.VMEM((2, 2 * DEVICES, N), bf16),
-            pltpu.VMEM((2, 2 * N, DEVICES), bf16),
+            pltpu.VMEM(mats.shape[1:], bf16),
+            pltpu.VMEM(mats.shape[1:], bf16),
+            pltpu.VMEM(inv.shape, bf16),
+            pltpu.VMEM(inv_t.shape, bf16),
             pltpu.VMEM((8, NZ, NZ), f32),
             pltpu.VMEM((8, NZ, NZ), bf16),
             pltpu.VMEM((8, NZ, NZ), bf16),
+            pltpu.VMEM((NZ, 2 * N), f32),
             pltpu.VMEM((NZ, 2 * N), bf16),
             pltpu.VMEM((NZ, 2 * N), bf16),
-            pltpu.VMEM((NZ, 2 * N), bf16),
-            pltpu.VMEM((NZ, 2 * N), bf16),
-            pltpu.VMEM((1, 2 * N), jnp.int32),
-            pltpu.VMEM((1, N), jnp.int32),
-            pltpu.VMEM((1, N), jnp.int32),
+            pltpu.VMEM((N, N), f32),
+            pltpu.VMEM((1, 2 * N), i32),
+            pltpu.VMEM((1, N), i32),
+            pltpu.VMEM((1, N), i32),
             pltpu.VMEM((32, 1, 128), f32),
             pltpu.VMEM((DEVICES, 1, 128), f32),
             pltpu.VMEM((N, 128), f32),
             pltpu.VMEM((4, 16, 128), f32),
-            dma((5,)),
+            pltpu.SemaphoreType.REGULAR,
+            dma((9,)),
+            dma,
+            dma((4,)),
+            dma,
+            dma((2,)),
         ]
-        + [dma] * 10,
+        + [dma] * 6,
         compiler_params=pltpu.CompilerParams(
             collective_id=0, has_side_effects=True, vmem_limit_bytes=48 * 1024 * 1024
         ),
     )(charge, fwd, shells, planes, green, mats, mats_t, inv, inv_t)
+    return field, jnp.transpose(plates, (0, 2, 1))
 
 
 def solution(mesh):

time: 85 us -> 77.3 us (0.909)
  Pallas kernels: 76.1 us -> 68.4 us
    pallas_call x1, Pallas kernels: 76.1 us -> 68.4 us  [local(): pl.pallas_call(kernel, out_shape=(jax.ShapeDtypeStruct(charge.shape, f32)...]
    unnamed x13 -> x14, local copies, waits for them, and re-layouts: 7.27 us -> 7.89 us
where the time goes in v3:
time: 77.3 us; the launch traced here: 77 us
  Pallas kernels  68.4 us (88%)
  local copies, waits for them, and re-layouts  7.89 us (10%)
    pallas_call x1, Pallas kernels, local(): pl.pallas_call(kernel, out_shape=(jax.ShapeDtypeStruct(charge.shape, f32)...  68.4 us
    unnamed x14, local copies, waits for them, and re-layouts  7.89 us

profile of v3, /device:TPU:1, one launch (start us, length us, event | category | flops | bytes accessed | tf_op | source)
XLA Modules:
  0.0 77.0 jit_solution(1420894568126045312)
XLA Ops:
  0.6 0.0 copy-start
  0.6 1.2 %copy-done = f32[64,8,512]{2,1,0:T(8,128)S(1)} copy-done((f32[64,8,512]{2,1,0:T(8,128)S(1)}, f32[64,8,512]{2,1,0:T(8,128)}, u32[]{:S(2)}) %copy-start) | copy-done | bytes 1048600
  1.9 0.0 copy-start.1
  1.9 1.2 %copy-done.1 = bf16[2,1024,256]{2,1,0:T(8,128)(2,1)S(1)} copy-done((bf16[2,1024,256]{2,1,0:T(8,128)(2,1)S(1)}, bf16[2,1024,256]{2,1,0:T(8,128)(2,1)}, u32[]{:S(2)}) %copy-start.1) | copy-done | bytes 1048600
  3.1 0.0 copy-start.2
  3.1 1.2 %copy-done.2 = bf16[2,2,256,512]{3,2,1,0:T(8,128)(2,1)S(1)} copy-done((bf16[2,2,256,512]{3,2,1,0:T(8,128)(2,1)S(1)}, bf16[2,2,256,512]{3,2,1,0:T(8,128)(2,1)}, u32[]{:S(2)}) %copy-start.2) | copy-done | bytes 1048600
  4.3 0.0 copy-start.3
  4.3 1.2 %copy-done.3 = bf16[2,512,512]{2,1,0:T(8,128)(2,1)S(1)} copy-done((bf16[2,512,512]{2,1,0:T(8,128)(2,1)S(1)}, bf16[2,512,512]{2,1,0:T(8,128)(2,1)}, u32[]{:S(2)}) %copy-start.3) | copy-done | bytes 1048600
  5.5 0.0 copy-start.4
  5.5 0.8 copy-done.4
  6.3 0.0 copy-start.5
  6.3 0.7 copy-done.5
  6.9 68.4 %shard_map.104 = (f32[64,8,512]{2,1,0:T(8,128)S(1)}, f32[4,16,64]{2,1,0:T(8,128)S(1)}) custom-call(f32[64,8,512]{2,1,0:T(8,128)S(1)} %copy-done, bf16[2,512,512]{2,1,0:T(8,128)(2,1)S(1)} %copy-done.3, s32[16,512]{1,0:T(8,128)S(1)} %copy-done.4, s32[4]{0:T(128)S(1)} %copy-done.5, f32[8,256,256]{2,1,0:T(8,128)} %green.1, ...), custom_call_target="tpu_custom_call" | custom-call | tf_op jit(solution)/shard_map/pallas_call | solution.py:325
  75.4 1.0 %copy.13 = f32[64,8,512]{2,1,0:T(8,128)} copy(f32[64,8,512]{2,1,0:T(8,128)S(1)} %get-tuple-element.8) | data formatting | bytes 2097152
  76.3 0.6 copy.14
Async XLA Ops:
  0.6 1.2 %copy-start = (f32[64,8,512]{2,1,0:T(8,128)S(1)}, f32[64,8,512]{2,1,0:T(8,128)}, u32[]{:S(2)}) copy-start(f32[64,8,512]{2,1,0:T(8,128)} %charge_h.1) | copy-start | bytes 3145732
  1.9 1.2 %copy-start.1 = (bf16[2,1024,256]{2,1,0:T(8,128)(2,1)S(1)}, bf16[2,1024,256]{2,1,0:T(8,128)(2,1)}, u32[]{:S(2)}) copy-start(bf16[2,1024,256]{2,1,0:T(8,128)(2,1)} %constant.14.clone.inv_t) | copy-start | bytes 3145732
  3.1 1.2 %copy-start.2 = (bf16[2,2,256,512]{3,2,1,0:T(8,128)(2,1)S(1)}, bf16[2,2,256,512]{3,2,1,0:T(8,128)(2,1)}, u32[]{:S(2)}) copy-start(bf16[2,2,256,512]{3,2,1,0:T(8,128)(2,1)} %constant.13.clone.inv) | copy-start | bytes 3145732
  4.3 1.2 %copy-start.3 = (bf16[2,512,512]{2,1,0:T(8,128)(2,1)S(1)}, bf16[2,512,512]{2,1,0:T(8,128)(2,1)}, u32[]{:S(2)}) copy-start(bf16[2,512,512]{2,1,0:T(8,128)(2,1)} %constant.10.clone.fwd_h) | copy-start | bytes 3145732
  5.5 0.8 copy-start.4
  6.3 0.7 copy-start.5

commit v4 on v3

--- a/solution.py
+++ b/solution.py
@@ -228,43 +228,39 @@
     lax.fori_loop(0, 4, solve, 0)
 
     spot = core * HALF + pair
-
-    def give(t, carry):
-        g = lax.rem(y + t, 4)
-        cols = pl.ds(pl.multiple_of(g * 256, 256), 256)
+    for g in range(4):
+        cols = slice(g * 256, (g + 1) * 256)
         back = dot3(v_hi[...], v_lo[...], mat_t[0, :, cols], mat_t[1, :, cols])
         for h in range(2):
-            obuf[pl.ds(pl.multiple_of((2 * g + h) * NZ, NZ), NZ), :] = back[:, h * 128 : (h + 1) * 128]
-        for h in range(2):
-            for p in range(4):
-                k = (2 * g + h) * 4 + p
-                ebuf[k] = obuf[pl.ds((2 * g + h) * NZ + planes[p], 1), :]
-                d = (2 * g + h) * BULKS + HOT * p
-
-                @pl.when(d != m)
-                def _():
-                    push(ebuf.at[k], erecv.at[m], d, essem, ersem).start()
-
-                @pl.when(d == m)
-                def _():
-                    pltpu.make_async_copy(ebuf.at[k], erecv.at[m], ersem).start()
-
-        @pl.when(t == 0)
+            obuf[(2 * g + h) * NZ : (2 * g + h + 1) * NZ, :] = back[:, h * 128 : (h + 1) * 128]
+
+    pltpu.make_async_copy(tile(obuf, m), tile(home, spot), hrsem.at[core]).start()
+
+    def give(i, carry):
+        d = lax.rem(m + i, DEVICES)
+        push(tile(obuf, d), tile(home, spot), d, hssem, hrsem.at[core]).start()
+        return carry
+
+    lax.fori_loop(1, 32, give, 0)
+    for g in range(ROWS):
+        for p in range(4):
+            ebuf[4 * g + p] = obuf[pl.ds(g * NZ + planes[p], 1), :]
+
+    def plate(k, carry):
+        d = lax.div(k, 4) * BULKS + HOT * lax.rem(k, 4)
+
+        @pl.when(d != m)
         def _():
-            pltpu.make_async_copy(tile(obuf, m), tile(home, spot), hrsem.at[core]).start()
-            d = m + 1 - 2 * core
-            push(tile(obuf, d), tile(home, spot), d, hssem, hrsem.at[core]).start()
-
-        def send(j, c):
-            d = 2 * (g * 32 + lax.rem(q0 + j, 32))
-            push(tile(obuf, d), tile(home, spot), d, hssem, hrsem.at[core]).start()
-            push(tile(obuf, d + 1), tile(home, spot), d + 1, hssem, hrsem.at[core]).start()
-            return c
-
-        lax.fori_loop(jnp.where(t == 0, 1, 0), 32, send, 0)
+            push(ebuf.at[k], erecv.at[m], d, essem, ersem).start()
+
+        @pl.when(d == m)
+        def _():
+            pltpu.make_async_copy(ebuf.at[k], erecv.at[m], ersem).start()
+
         return carry
 
-    lax.fori_loop(0, 4, give, 0)
+    lax.fori_loop(0, 32, plate, 0)
+    lax.fori_loop(32, DEVICES, give, 0)
     loads[7].wait()
     loads[8].wait()
 
@@ -322,6 +318,7 @@
     f32, bf16, i32 = jnp.float32, jnp.bfloat16, jnp.int32
     vmem, hbm = pl.BlockSpec(memory_space=pltpu.VMEM), pl.BlockSpec(memory_space=pltpu.HBM)
     dma = pltpu.SemaphoreType.DMA
+    operands = (charge, fwd, shells, planes, green, mats, mats_t, inv, inv_t)
     field, plates = pl.pallas_call(
         kernel,
         out_shape=(
@@ -368,7 +365,7 @@
         compiler_params=pltpu.CompilerParams(
             collective_id=0, has_side_effects=True, vmem_limit_bytes=48 * 1024 * 1024
         ),
-    )(charge, fwd, shells, planes, green, mats, mats_t, inv, inv_t)
+    )(*(pltpu.with_memory_space_constraint(a, pltpu.HBM) for a in operands))
     return field, jnp.transpose(plates, (0, 2, 1))
 
 

time: 77.3 us -> 67 us (0.87)
  local copies, waits for them, and re-layouts: 7.89 us -> 1.59 us
  Pallas kernels: 68.4 us -> 64.7 us
    unnamed x14 -> x2, local copies, waits for them, and re-layouts: 7.89 us -> 1.59 us
    pallas_call x1, Pallas kernels: 68.4 us -> 64.7 us  [local(): pl.pallas_call(kernel, out_shape=(jax.ShapeDtypeStruct(charge.shape, f32)...]
where the time goes in v4:
time: 67 us; the launch traced here: 66.9 us
  Pallas kernels  64.7 us (97%)
  local copies, waits for them, and re-layouts  1.59 us (2%)
    pallas_call x1, Pallas kernels, local(): pl.pallas_call(kernel, out_shape=(jax.ShapeDtypeStruct(charge.shape, f32)...  64.7 us
    unnamed x2, local copies, waits for them, and re-layouts  1.59 us

profile of v4, /device:TPU:1, one launch (start us, length us, event | category | flops | bytes accessed | tf_op | source)
XLA Modules:
  0.0 66.9 jit_solution(8787567690831147832)
XLA Ops:
  0.6 64.7 %shard_map.104 = (f32[64,8,512]{2,1,0:T(8,128)S(1)}, f32[4,16,64]{2,1,0:T(8,128)S(1)}) custom-call(f32[64,8,512]{2,1,0:T(8,128)} %charge_h.1, bf16[2,512,512]{2,1,0:T(8,128)(2,1)} %constant.10.clone.fwd_h, s32[16,512]{1,0:T(8,128)} %shells_h.1, s32[4]{0:T(128)} %planes_h.1, f32[8,256,256]{2,1,0:T(8,128)} %green.1, ...), custom_call_target="tpu_custom_call" | custom-call | tf_op jit(solution)/shard_map/pallas_call | solution.py:322
  65.4 1.0 %copy.13 = f32[64,8,512]{2,1,0:T(8,128)} copy(f32[64,8,512]{2,1,0:T(8,128)S(1)} %get-tuple-element.8) | data formatting | bytes 2097152
  66.3 0.6 copy.14

commit v5 on v4

--- a/solution.py
+++ b/solution.py
@@ -123,12 +123,12 @@
     x = lax.div(b, 8)
 
     def place(px, py, pz, pc):
-        return {"row": py * 2 + lax.div(pz, 4), "bulk": px * 8 + lax.rem(pz, 4) * 2 + pc}
+        return (py * 2 + lax.div(pz, 4)) * BULKS + px * 8 + lax.rem(pz, 4) * 2 + pc
 
     plane_peers = [place(lax.rem(x + i, 4), lax.rem(y + j, 4), z, core) for i in range(4) for j in range(4) if i + j]
     line_peers = [place(x, y, lax.rem(z + i, 8), lax.rem(core + j, 2)) for i in range(8) for j in range(2) if i + j]
     for peer in plane_peers + line_peers:
-        pl.semaphore_signal(barrier, inc=1, device_id=peer, device_id_type=MESH)
+        pl.semaphore_signal(barrier, inc=1, device_id=at(peer), device_id_type=MESH)
     for load in loads[4:]:
         load.start()
 
@@ -136,6 +136,10 @@
     loads[1].wait()
     lane = lax.broadcasted_iota(jnp.int32, (DEVICES, 128), 1)
     for q in range(2):
+        if q == 1:
+            pl.semaphore_wait(barrier, len(plane_peers) + len(line_peers))
+            for peer in line_peers:
+                pl.semaphore_signal(gate, inc=1, device_id=at(peer), device_id_type=MESH)
         rows = jnp.concatenate([charge[:, 4 * q + j, :] for j in range(4)], axis=0)
         c_hi, c_lo = parts(rows)
         spec = dot3(fwd[0], fwd[1], c_hi, c_lo, ((1,), (1,)))
@@ -151,26 +155,26 @@
     lab[:, :N] = shells[pl.ds(jnp.where(b < BULKS // 2, r, 8 - r), 1), :]
     lab_src[...] = shells[0:1, :]
 
-    pl.semaphore_wait(barrier, len(plane_peers) + len(line_peers))
-    for peer in line_peers:
-        pl.semaphore_signal(gate, inc=1, device_id=peer, device_id_type=MESH)
+    pltpu.make_async_copy(tile(sbuf, m), tile(rbuf, m), rsem.at[y]).start()
+
+    def send(d):
+        push(tile(sbuf, d), tile(rbuf, m), d, ssem, rsem.at[y]).start()
+
+    for peer in line_peers + plane_peers:
+        send(peer)
     pl.semaphore_wait(gate, len(line_peers))
-
-    pltpu.make_async_copy(tile(sbuf, m), tile(rbuf, m), rsem.at[y]).start()
     for c in range(2):
-
-        @pl.when(core != c)
-        def _(c=c):
-            d = 2 * pair + c
-            push(tile(sbuf, d), tile(rbuf, m), d, ssem, rsem.at[y]).start()
-
-        def send(i, carry, c=c):
-            t, j = lax.div(i, 32), lax.rem(i, 32)
-            d = 2 * (lax.rem(y + t, 4) * 32 + lax.rem(q0 + j, 32)) + c
-            push(tile(sbuf, d), tile(rbuf, m), d, ssem, rsem.at[y]).start()
-            return carry
-
-        lax.fori_loop(1, HALF, send, 0)
+        def across(k, carry, c=c):
+            base = lax.rem(y + lax.div(k, 4), 4) * 2 * BULKS + lax.rem(x + lax.rem(k, 4), 4) * 8 + c
+
+            def along(j, inner):
+                pz = lax.rem(z + j, 8)
+                send(base + lax.div(pz, 4) * BULKS + lax.rem(pz, 4) * 2)
+                return inner
+
+            return lax.fori_loop(jnp.where(core == c, 1, 0), 8, along, carry)
+
+        lax.fori_loop(1, 16, across, 0)
 
     @pl.when(feeder)
     def _():
@@ -281,16 +285,18 @@
         drain(erecv, ersem)
         e_hi, e_lo = parts(erecv[...].reshape(DEVICES, 128))
         both = dot3(inv_t_v[0], inv_t_v[1], e_hi, e_lo)
-        eout[...] = both[:N] + pltpu.roll(both[N:], 64, 1)
+        near = (both[:N] + pltpu.roll(both[N:], 64, 1)).reshape(BULKS, 16, 128)
+        far = (pltpu.roll(both[:N], 64, 1) + both[N:]).reshape(BULKS, 16, 128)
+        side = lax.broadcasted_iota(jnp.int32, (BULKS, 8, 128), 2)
+        eout[...] = jnp.where(side < 64, near[:, :8], far[:, 8:]).reshape(8 * BULKS, 128)
         p = lax.div(b, HOT)
 
         def spread(j, c):
             d = r * BULKS + lax.rem(b + j, BULKS)
-            src = eout.at[pl.ds(pl.multiple_of(lax.rem(d, BULKS) * 16, 16), 16), :]
-            push(src, elrecv.at[p], d, elssem, elrsem).start()
+            push(tile(eout, lax.rem(d, BULKS)), elrecv.at[p], d, elssem, elrsem).start()
             return c
 
-        pltpu.make_async_copy(eout.at[pl.ds(pl.multiple_of(b * 16, 16), 16), :], elrecv.at[p], elrsem).start()
+        pltpu.make_async_copy(tile(eout, b), elrecv.at[p], elrsem).start()
         lax.fori_loop(1, BULKS, spread, 0)
 
     rest = regain(1)
@@ -298,7 +304,8 @@
         out[:, k, :] = field_ref[64 * k : 64 * (k + 1), :] + rest[64 * k : 64 * (k + 1)]
 
     drain(elrecv, elrsem)
-    electrodes[...] = elrecv[:, :, :64]
+    electrodes[:, :8, :] = elrecv[:, :, :64]
+    electrodes[:, 8:, :] = elrecv[:, :, 64:]
 
     drain(sbuf.at[pl.ds(0, 8 * (DEVICES - 1)), :], ssem)
     drain(obuf.at[pl.ds(0, 8 * (DEVICES - 1)), :], hssem)
@@ -310,7 +317,7 @@
 
     @pl.when(hot)
     def _():
-        drain(eout.at[pl.ds(0, 16 * (BULKS - 1)), :], elssem)
+        drain(eout.at[pl.ds(0, 8 * (BULKS - 1)), :], elssem)
 
 
 def local(charge, green, shells, planes):
@@ -352,8 +359,8 @@
             pltpu.VMEM((1, N), i32),
             pltpu.VMEM((32, 1, 128), f32),
             pltpu.VMEM((DEVICES, 1, 128), f32),
-            pltpu.VMEM((N, 128), f32),
-            pltpu.VMEM((4, 16, 128), f32),
+            pltpu.VMEM((8 * BULKS, 128), f32),
+            pltpu.VMEM((4, 8, 128), f32),
             pltpu.SemaphoreType.REGULAR,
             dma((9,)),
             dma,

time: 67 us -> 66.4 us (level)
  Pallas kernels: 64.7 us -> 64 us
    pallas_call x1, Pallas kernels: 64.7 us -> 64 us  [local(): pl.pallas_call(kernel, out_shape=(jax.ShapeDtypeStruct(charge.shape, f32)...]
where the time goes in v5:
time: 66.4 us; the launch traced here: 66.2 us
  Pallas kernels  64 us (96%)
  local copies, waits for them, and re-layouts  1.59 us (2%)
    pallas_call x1, Pallas kernels, local(): pl.pallas_call(kernel, out_shape=(jax.ShapeDtypeStruct(charge.shape, f32)...  64 us
    unnamed x2, local copies, waits for them, and re-layouts  1.59 us

profile of v5, /device:TPU:1, one launch (start us, length us, event | category | flops | bytes accessed | tf_op | source)
XLA Modules:
  0.0 66.2 jit_solution(11865385831515268363)
XLA Ops:
  0.6 64.0 %shard_map.104 = (f32[64,8,512]{2,1,0:T(8,128)S(1)}, f32[4,16,64]{2,1,0:T(8,128)S(1)}) custom-call(f32[64,8,512]{2,1,0:T(8,128)} %charge_h.1, bf16[2,512,512]{2,1,0:T(8,128)(2,1)} %constant.10.clone.fwd_h, s32[16,512]{1,0:T(8,128)} %shells_h.1, s32[4]{0:T(128)} %planes_h.1, f32[8,256,256]{2,1,0:T(8,128)} %green.1, ...), custom_call_target="tpu_custom_call" | custom-call | tf_op jit(solution)/shard_map/pallas_call | solution.py:329
  64.6 1.0 %copy.13 = f32[64,8,512]{2,1,0:T(8,128)} copy(f32[64,8,512]{2,1,0:T(8,128)S(1)} %get-tuple-element.8) | data formatting | bytes 2097152
  65.6 0.6 copy.14

commit v6 on v5

--- a/solution.py
+++ b/solution.py
@@ -136,13 +136,13 @@
     loads[1].wait()
     lane = lax.broadcasted_iota(jnp.int32, (DEVICES, 128), 1)
     for q in range(2):
+        rows = jnp.concatenate([charge[:, 4 * q + j, :] for j in range(4)], axis=0)
+        c_hi, c_lo = parts(rows)
+        spec = dot3(fwd[0], fwd[1], c_hi, c_lo, ((1,), (1,)))
         if q == 1:
             pl.semaphore_wait(barrier, len(plane_peers) + len(line_peers))
             for peer in line_peers:
                 pl.semaphore_signal(gate, inc=1, device_id=at(peer), device_id_type=MESH)
-        rows = jnp.concatenate([charge[:, 4 * q + j, :] for j in range(4)], axis=0)
-        c_hi, c_lo = parts(rows)
-        spec = dot3(fwd[0], fwd[1], c_hi, c_lo, ((1,), (1,)))
         for p in range(2):
             re = spec[:DEVICES, 128 * p : 128 * (p + 1)]
             im = spec[DEVICES:, 128 * p : 128 * (p + 1)]
@@ -212,7 +212,7 @@
         spec_ref[...] += dot3(hi, lo, mat[0, deep, :], mat[1, deep, :])
         return carry
 
-    lax.fori_loop(0, 4, gather, 0)
+    lax.fori_loop(0, 4, gather, 0, unroll=True)
 
     def solve(t, carry):
         cols = pl.ds(pl.multiple_of(t * 256, 256), 256)
@@ -229,7 +229,7 @@
         v_lo[:, cols] = lo
         return carry
 
-    lax.fori_loop(0, 4, solve, 0)
+    lax.fori_loop(0, 4, solve, 0, unroll=True)
 
     spot = core * HALF + pair
     for g in range(4):

time: 66.4 us -> 65.4 us (0.985)
  Pallas kernels: 64 us -> 63.1 us
    pallas_call x1, Pallas kernels: 64 us -> 63.1 us  [local(): pl.pallas_call(kernel, out_shape=(jax.ShapeDtypeStruct(charge.shape, f32)...]
where the time goes in v6:
time: 65.4 us; the launch traced here: 65.3 us
  Pallas kernels  63.1 us (96%)
  local copies, waits for them, and re-layouts  1.59 us (2%)
    pallas_call x1, Pallas kernels, local(): pl.pallas_call(kernel, out_shape=(jax.ShapeDtypeStruct(charge.shape, f32)...  63.1 us
    unnamed x2, local copies, waits for them, and re-layouts  1.59 us

profile of v6, /device:TPU:1, one launch (start us, length us, event | category | flops | bytes accessed | tf_op | source)
XLA Modules:
  0.0 65.3 jit_solution(4359746933314283155)
XLA Ops:
  0.6 63.1 %shard_map.104 = (f32[64,8,512]{2,1,0:T(8,128)S(1)}, f32[4,16,64]{2,1,0:T(8,128)S(1)}) custom-call(f32[64,8,512]{2,1,0:T(8,128)} %charge_h.1, bf16[2,512,512]{2,1,0:T(8,128)(2,1)} %constant.10.clone.fwd_h, s32[16,512]{1,0:T(8,128)} %shells_h.1, s32[4]{0:T(128)} %planes_h.1, f32[8,256,256]{2,1,0:T(8,128)} %green.1, ...), custom_call_target="tpu_custom_call" | custom-call | tf_op jit(solution)/shard_map/pallas_call | solution.py:329
  63.7 1.0 %copy.13 = f32[64,8,512]{2,1,0:T(8,128)} copy(f32[64,8,512]{2,1,0:T(8,128)S(1)} %get-tuple-element.8) | data formatting | bytes 2097152
  64.7 0.6 copy.14

commit v7 on v6

--- a/solution.py
+++ b/solution.py
@@ -232,11 +232,11 @@
     lax.fori_loop(0, 4, solve, 0, unroll=True)
 
     spot = core * HALF + pair
-    for g in range(4):
-        cols = slice(g * 256, (g + 1) * 256)
+    for g in range(2):
+        cols = slice(g * 512, (g + 1) * 512)
         back = dot3(v_hi[...], v_lo[...], mat_t[0, :, cols], mat_t[1, :, cols])
-        for h in range(2):
-            obuf[(2 * g + h) * NZ : (2 * g + h + 1) * NZ, :] = back[:, h * 128 : (h + 1) * 128]
+        for h in range(4):
+            obuf[(4 * g + h) * NZ : (4 * g + h + 1) * NZ, :] = back[:, h * 128 : (h + 1) * 128]
 
     pltpu.make_async_copy(tile(obuf, m), tile(home, spot), hrsem.at[core]).start()
 
@@ -263,8 +263,8 @@
 
         return carry
 
-    lax.fori_loop(0, 32, plate, 0)
-    lax.fori_loop(32, DEVICES, give, 0)
+    lax.fori_loop(0, 32, plate, 0, unroll=4)
+    lax.fori_loop(32, DEVICES, give, 0, unroll=4)
     loads[7].wait()
     loads[8].wait()
 

time: 65.4 us -> 65.2 us (level)
  no operation moved by 1% of the time
where the time goes in v7:
time: 65.2 us; the launch traced here: 65.1 us
  Pallas kernels  62.9 us (96%)
  local copies, waits for them, and re-layouts  1.59 us (2%)
    pallas_call x1, Pallas kernels, local(): pl.pallas_call(kernel, out_shape=(jax.ShapeDtypeStruct(charge.shape, f32)...  62.9 us
    unnamed x2, local copies, waits for them, and re-layouts  1.59 us

profile of v7, /device:TPU:1, one launch (start us, length us, event | category | flops | bytes accessed | tf_op | source)
XLA Modules:
  0.0 65.1 jit_solution(17705255630667117783)
XLA Ops:
  0.6 62.9 %shard_map.104 = (f32[64,8,512]{2,1,0:T(8,128)S(1)}, f32[4,16,64]{2,1,0:T(8,128)S(1)}) custom-call(f32[64,8,512]{2,1,0:T(8,128)} %charge_h.1, bf16[2,512,512]{2,1,0:T(8,128)(2,1)} %constant.10.clone.fwd_h, s32[16,512]{1,0:T(8,128)} %shells_h.1, s32[4]{0:T(128)} %planes_h.1, f32[8,256,256]{2,1,0:T(8,128)} %green.1, ...), custom_call_target="tpu_custom_call" | custom-call | tf_op jit(solution)/shard_map/pallas_call | solution.py:329
  63.5 1.0 %copy.13 = f32[64,8,512]{2,1,0:T(8,128)} copy(f32[64,8,512]{2,1,0:T(8,128)S(1)} %get-tuple-element.8) | data formatting | bytes 2097152
  64.5 0.6 copy.14
